TPU v7x, 32 devices: a whole 2x2x4 slice. The times are simulated.
32 devices in a mesh: gx: 2 (over y), gy: 4 (over z), gz: 4 (over x, core).
Axes of the slice: x: 2, y: 2, z: 4, core: 2. Of those that a mesh axis runs over, the one named last changes fastest.
Arguments:
- tensor: float32 [256, 512, 512], P('gx', 'gy', 'gz'), may hold values from -0.75 to 0.75
- factor_a: float32 [256, 256], P(('gy', 'gz'), 'gx'), may hold values from -1.7 to 1.7
- factor_b: float32 [256, 512], P(('gx', 'gz'), 'gy'), may hold values from -1.7 to 1.7
- factor_c: float32 [256, 512], P(('gx', 'gy'), 'gz'), may hold values from -1.7 to 1.7
Outputs:
- grad_a: float32 [256, 256], P(('gy', 'gz'), 'gx')
- grad_b: float32 [256, 512], P(('gx', 'gz'), 'gy')
- grad_c: float32 [256, 512], P(('gx', 'gy'), 'gz')
All inputs are finite; a program needn't handle non-finite values.
Results may differ from a plain program's by a relative error of at most 0.00019.
Values sent between devices are 32-bit elements; how exact they have to be, the bound alone decides.
No kernel may reach another device: no remote copies, remote signals or barrier semaphores. Data moves between devices by JAX's collectives and lax.ppermute only.
A program may use at most 128 MiB of HBM per device.

v0:
```python
import jax
import jax.numpy as jnp
from jax import lax
from jax.experimental import pallas as pl
from jax.experimental.pallas import tpu as pltpu
from jax.sharding import PartitionSpec as P

R = 64
PAIR = 2 * R
GROUP = 8
UNROLL = 8
BUFFERS = 4
TILE = 8
TURNS = 16
MIB = 1024 * 1024


def split(value):
    high = value.astype(jnp.bfloat16)
    low = (value - high.astype(jnp.float32)).astype(jnp.bfloat16)
    return high, low


def pair_grams(rows):
    row = lax.broadcasted_iota(jnp.int32, (PAIR, PAIR), 0) // R
    col = lax.broadcasted_iota(jnp.int32, (PAIR, PAIR), 1) // R
    blocks = []
    for pair in range(rows.shape[0] // PAIR):
        part = rows[pair * PAIR : (pair + 1) * PAIR, :]
        high, low = split(part)
        gram = lax.dot_general(
            jnp.concatenate([high, low, high], axis=1),
            jnp.concatenate([high, high, low], axis=1),
            (((1,), (1,)), ((), ())),
            preferred_element_type=jnp.float32,
        )
        blocks.append(folded(jnp.where(row == col, gram, 0.0)))
    return jnp.concatenate(blocks, axis=0)


def folded(value):
    half = value.shape[1] // 2
    return value + jnp.concatenate([value[:, half:], value[:, :half]], axis=1)


def packs(rows):
    return rows % 16 == 0


def packed_rows(rows):
    return rows // 2 if packs(rows) else rows


def packed(gram, rows):
    blocks = gram.reshape(-1, rows, gram.shape[1])
    if not packs(rows):
        return blocks
    half = rows // 2
    lane = lax.broadcasted_iota(jnp.int32, (blocks.shape[0], half, gram.shape[1]), 2)
    return jnp.where(lane < R, blocks[:, :half], blocks[:, half:])


def unpacked(block, rows):
    if not packs(rows):
        return block
    lane = lax.broadcasted_iota(jnp.int32, block.shape, 1)
    return folded(jnp.concatenate([jnp.where(lane < R, block, 0.0), jnp.where(lane < R, 0.0, block)], axis=0))


def here():
    return lax.axis_index("gx"), lax.axis_index("gy"), lax.axis_index("gz")


def take(refs, *counts):
    groups, first = [], 0
    for count in counts:
        groups.append(refs[first : first + count])
        first += count
    return groups, refs[first:]


def put(ref, values):
    first = 0
    for value in values:
        ref[first : first + value.shape[0], :] = value
        first += value.shape[0]


def total_of(refs):
    total = refs[0][...]
    for ref in refs[1:]:
        total = total + ref[...]
    return total


def own_kernel(sizes, a_ref, b_ref, c_ref, ac_ref, own_b, sems):
    ra = a_ref.shape[0]
    targets = [ac_ref.at[:ra], own_b, ac_ref.at[ra:]]
    copies = [
        pltpu.make_async_copy(source, target, sems.at[n])
        for n, (source, target) in enumerate(zip([a_ref, b_ref, c_ref], targets))
    ]
    for copy in copies:
        copy.start()
    for copy in copies:
        copy.wait()


def pack_kernel(sizes, *refs):
    nx, ny, nz, ra, rb, rc = sizes
    (ac, (b, for_z, for_x)), _ = take(refs, ny, 3)
    put(for_z, [ref[:ra, :] for ref in ac] + [b[...]])
    put(for_x, [ref[ra:, :] for ref in ac])


def sweep(blocks, contract, reduce, results):
    @pl.loop(0, blocks // UNROLL)
    def _(turn):
        for n in range(UNROLL + 1):
            if n < UNROLL:
                contract(turn, n, results[n % BUFFERS])
            if n:
                reduce(turn, n - 1, results[(n - 1) % BUFFERS])


def spread(counts, turn, n):
    turns = sum(counts) // (GROUP * UNROLL)
    first = 0
    for array, count in enumerate(counts):
        share = count // (GROUP * turns)
        if n < share:
            start = (turn * share + n) * GROUP
            return array, pl.multiple_of(start, GROUP), pl.multiple_of(first + start, GROUP)
        n -= share
        first += count


def weights(columns):
    both = jnp.concatenate(split(columns), axis=1)
    return jnp.concatenate([both, both], axis=0)


def product(pair, weights):
    value = jnp.dot(pair, weights, preferred_element_type=jnp.float32)
    half = value.shape[1] // 2
    return value[:, :half] + value[:, half:]


def accurate(rows, columns):
    return product(jnp.concatenate(split(rows), axis=1), weights(columns))


def flat(block):
    return block.reshape(block.shape[0] * block.shape[1], block.shape[2])


def transpose(pairs, first, turned, start, count):
    for n in range(count):
        turned[start + n] = transposed(pairs[first + n])


def transposed(pair):
    half = pair.shape[1] // 2
    return jnp.concatenate([pair[:, :half].T, pair[:, half:].T], axis=1)


def tensor_kernel(sizes, *refs):
    (b, (tensor, pairs, turned, rows_b)), _ = take(refs, sizes[0], 4)
    put(rows_b, [ref[...] for ref in b])

    @pl.loop(0, tensor.shape[0] // (2 * TURNS))
    def _(turn):
        for n in range(2 * TURNS):
            place = turn * 2 * TURNS + n
            pair = jnp.concatenate(split(tensor[place]), axis=1)
            pairs[place] = pair
        for n in range(TURNS):
            transpose(pairs, turn * TURNS + n, turned, turn * TURNS + n, 1)


def own_half(x, nx):
    return x // (nx // 2)


def early_columns(sizes, packs_x, c_ref):
    nx, ny, nz, ra, rb, rc = sizes
    x, y, z = here()
    part = lax.rem(x, nx // 2)
    for sx in range(nx // 2):
        for sy in range(ny):
            place = ((part ^ sx) * ny + (y ^ sy)) * rc
            c_ref[pl.ds(place, rc), :] = packs_x[sx][sy * rc : (sy + 1) * rc, :]


def early_loop(first, count, pairs, weights_ref, own_y, turned):
    nj = pairs.shape[1]
    turns = GROUP // 2
    start = pairs.shape[0] // 2 + first // 2
    for block in range(count // GROUP):
        own_y[pl.ds(block * GROUP * nj, GROUP * nj), :] = product(
            flat(pairs[pl.ds(first + block * GROUP, GROUP)]), weights_ref[...]
        )
        transpose(pairs, start + block * turns, turned, block * turns, turns)


def early_kernel(sizes, *refs):
    (packs_x, (pairs, own_y, turned, c_ref, cc_ref)), _ = take(refs, sizes[0] // 2, 5)
    early_columns(sizes, packs_x, c_ref)
    cc_ref[...] = weights(c_ref[...].T)
    early_loop(0, own_y.shape[0] // pairs.shape[1], pairs, cc_ref, own_y, turned)


def later_kernel(sizes, pairs, cc_ref, own_y, turned):
    count = own_y.shape[0] // pairs.shape[1]
    early_loop(pairs.shape[0] - count, count, pairs, cc_ref, own_y, turned)


def stack_kernel(sizes, *refs):
    *values, _, target = refs
    put(target, [value[...] for value in values])


def first_kernel(sizes, *refs):
    nx, ny, nz, ra, rb, rc = sizes
    (packs_z, packs_x, own_y, (own_c, pairs), sends), refs = take(refs, 2, nx // 2, 2, 2, 2)
    a_ref, at_ref, b_ref, c_ref, bt_ref, cc_ref, ma_ref, mb_ref = refs[:8]
    (ca_ref, cb_ref), results, (rows_of,) = refs[8:10], refs[10:-1], refs[-1:]
    pa, pb = packed_rows(ra), packed_rows(rb)
    x, y, z = here()
    ni, nj = pairs.shape[0], pairs.shape[1]
    lanes = c_ref.shape[0] // 2
    half = own_half(x, nx)
    own, other = half * lanes, (1 - half) * lanes

    for sz in range(nz):
        start = sz // 2 * (ny * ra + nx * rb)
        for sy in range(ny):
            a_ref[pl.ds(((y ^ sy) * nz + (z ^ sz)) * ra, ra), :] = packs_z[sz % 2][start : start + ra, :]
            start += ra
        for sx in range(nx):
            b_ref[pl.ds(((x ^ sx) * nz + (z ^ sz)) * rb, rb), :] = packs_z[sz % 2][start : start + rb, :]
            start += rb
    c_ref[pl.ds(own, lanes), :] = own_c[...]
    for sx in range(nx // 2):
        for sy in range(ny):
            place = ((x ^ (sx + nx // 2)) * ny + (y ^ sy)) * rc
            c_ref[pl.ds(place, rc), :] = packs_x[sx][sy * rc : (sy + 1) * rc, :]
    for n, first in enumerate((own, other)):
        at_ref[n] = a_ref[pl.ds(first, lanes), :].T
        bt_ref[n] = b_ref[pl.ds(first, lanes), :].T
    cc_ref[...] = weights(c_ref[pl.ds(other, lanes), :].T)
    gram = pair_grams(c_ref[...])
    ca_ref[...] = packed(gram, ra)
    cb_ref[...] = packed(gram, rb)
    mb_ref[...] = jnp.zeros_like(mb_ref)

    counts = [ref.shape[0] // nj for ref in own_y]

    def contract(turn, n, result):
        slices = spread(counts, turn, n)[2]
        result[...] = product(flat(pairs[pl.ds(slices, GROUP)]), cc_ref[...])

    def reduce(turn, n, result):
        part, start, first = spread(counts, turn, n)
        start = pl.multiple_of(start * nj, GROUP * nj)
        for n in range(2):
            scales = [jnp.broadcast_to(at_ref[n, pl.ds(first + g, 1), :], (TILE, lanes)) for g in range(GROUP)]
            sums = [jnp.zeros((TILE, lanes), jnp.float32)] * GROUP
            for tile in range(nj // TILE):
                rows = slice(tile * TILE, (tile + 1) * TILE)
                total = mb_ref[n, rows, :]
                across = bt_ref[n, rows, :]
                for g in range(GROUP):
                    place = g * nj + tile * TILE
                    if n == 0:
                        value = own_y[part][pl.ds(start + place, TILE), :]
                    else:
                        value = result[place : place + TILE, :]
                    total = total + scales[g] * value
                    sums[g] = sums[g] + across * value
                mb_ref[n, rows, :] = total
            for g in range(GROUP):
                ma_ref[n, pl.ds(first + g, 1), :] = jnp.sum(sums[g], axis=0, keepdims=True)

    sweep(ni // GROUP, contract, reduce, results)

    for n in range(2):
        rows_of[0, n * lanes : (n + 1) * lanes, :] = ma_ref[n].T
        rows_of[1, n * lanes : (n + 1) * lanes, :] = mb_ref[n].T
    for sz in range(nz):
        to_z = z ^ sz
        count = ny * ra + nx * rb + pa + pb
        put(
            sends[sz % 2].at[sz // 2 * count : (sz // 2 + 1) * count],
            [rows_of[0, pl.ds((((y ^ sy) * nz + to_z) * ra) ^ own, ra), :] for sy in range(ny)]
            + [rows_of[1, pl.ds((((x ^ sx) * nz + to_z) * rb) ^ own, rb), :] for sx in range(nx)]
            + [ca_ref[y * nz + to_z], cb_ref[x * nz + to_z]],
        )


def third_loop(turned, columns, weights_ref, result_refs, total_ref):
    total_ref[...] = jnp.zeros_like(total_ref)
    nk, lanes = total_ref.shape
    counts = [ref.shape[0] for ref in turned]

    def contract(turn, n, result):
        array, start, _ = spread(counts, turn, n)
        result[...] = product(flat(turned[array][pl.ds(start, GROUP)]), weights_ref[...])

    def reduce(turn, n, result):
        first = spread(counts, turn, n)[2]
        scales = [jnp.broadcast_to(columns[pl.ds(first + g, 1), :], (TILE, lanes)) for g in range(GROUP)]
        for tile in range(nk // TILE):
            rows = slice(tile * TILE, (tile + 1) * TILE)
            total = total_ref[rows, :]
            for g in range(GROUP):
                place = g * nk + tile * TILE
                total = total + scales[g] * result[place : place + TILE, :]
            total_ref[rows, :] = total

    sweep(sum(counts) // GROUP, contract, reduce, result_refs)


def partner_kernel(sizes, *refs):
    nx, ny, nz, ra, rb, rc = sizes
    (turned, (a_ref, at_ref, b_ref), sends), refs = take(refs, 3, 3, nx // 2)
    (kept_b, tb_ref, tc_ref, bb_ref, mc_ref, ba_ref, bc_ref), results, rows_of = refs[:7], refs[7:-1], refs[-1]
    x, y, z = here()
    lanes = mc_ref.shape[1]
    other = (1 - own_half(x, nx)) * lanes
    bb_ref[...] = weights(b_ref[pl.ds(other, lanes), :].T)
    gram = pair_grams(a_ref[...])
    tb_ref[...] = packed(gram, rb)
    tc_ref[...] = packed(gram, rc)
    gram = pair_grams(b_ref[...])
    ba_ref[...] = packed(gram, ra)
    bc_ref[...] = packed(gram, rc)
    third_loop(turned, at_ref.at[1], bb_ref, results, mc_ref)
    rows_of[...] = mc_ref[...].T
    for sx in range(nx // 2):
        to_x = x ^ (sx + nx // 2)
        put(
            sends[sx],
            [rows_of[pl.ds((to_x * ny + (y ^ sy)) * rc - other, rc), :] for sy in range(ny)]
            + [tb_ref[to_x * nz + z], tc_ref[to_x * ny + y]],
        )
    grams = []
    for sy in range(ny):
        grams += [ba_ref[(y ^ sy) * nz + z], bc_ref[x * ny + (y ^ sy)]]
    put(kept_b, grams)


def own_third_kernel(sizes, *refs):
    nx, ny, nz, ra, rb, rc = sizes
    (turned, (at_ref, b_ref, tb_ref, tc_ref), sends), refs = take(refs, 3, 4, nx // 2)
    (bb_ref, mc_ref), results, rows_of = refs[:2], refs[2:-1], refs[-1]
    x, y, z = here()
    lanes = mc_ref.shape[1]
    own = own_half(x, nx) * lanes
    bb_ref[...] = weights(b_ref[pl.ds(own, lanes), :].T)
    third_loop(turned, at_ref.at[0], bb_ref, results, mc_ref)
    rows_of[...] = mc_ref[...].T
    for sx in range(nx // 2):
        to_x = x ^ sx
        put(
            sends[sx],
            [rows_of[pl.ds((to_x * ny + (y ^ sy)) * rc - own, rc), :] for sy in range(ny)]
            + [tb_ref[to_x * nz + z], tc_ref[to_x * ny + y]],
        )


def core_kernel(sizes, own, other, *outs):
    count = outs[0].shape[0]
    for part, out in enumerate(outs):
        rows = slice(part * count, (part + 1) * count)
        out[...] = own[rows, :] + other[rows, :]


def middle_kernel(sizes, *refs):
    nx, ny, nz, ra, rb, rc = sizes
    (from_z, from_x, (grams_b,), for_y, for_x), (kept,) = take(refs, nz // 2, nx, 1, ny, nx)
    pa, pb, pc = packed_rows(ra), packed_rows(rb), packed_rows(rc)
    sum_z, sum_x = total_of(from_z), total_of(from_x)
    for sy in range(ny):
        put(
            for_y[sy],
            [
                sum_z[sy * ra : (sy + 1) * ra],
                sum_x[sy * rc : (sy + 1) * rc],
                grams_b[sy * (pa + pc) : (sy + 1) * (pa + pc), :],
            ],
        )
    for sx in range(nx):
        for_x[sx][...] = sum_z[ny * ra + sx * rb : ny * ra + (sx + 1) * rb]
    put(kept, [sum_z[ny * ra + nx * rb :], sum_x[ny * rc :]])


def scaled(one, other, rows, factor_ref, first_row):
    hessian = unpacked(one * other, rows)
    lane = lax.broadcasted_iota(jnp.int32, hessian.shape, 1)
    hessian = jnp.where(lane // R == lax.rem(first_row // R, 2), hessian, 0.0)
    pair = pl.multiple_of(first_row // PAIR * PAIR, PAIR)
    return accurate(hessian, factor_ref[pl.ds(pair, PAIR), :])


def grad_b_kernel(sizes, *refs):
    nx, ny, nz, ra, rb, rc = sizes
    (from_x, (kept, b_ref, grad_b)), _ = take(refs, nx, 3)
    pa, pb = packed_rows(ra), packed_rows(rb)
    x, y, z = here()
    gram_cb, gram_ab = kept[pa : pa + pb, :], kept[pa + pb : pa + 2 * pb, :]
    grad_b[...] = scaled(gram_ab, gram_cb, rb, b_ref, (x * nz + z) * rb) - total_of(from_x)


def last_kernel(sizes, *refs):
    nx, ny, nz, ra, rb, rc = sizes
    (from_y, (kept, a_ref, c_ref, grad_a, grad_c)), _ = take(refs, ny, 5)
    pa, pb = packed_rows(ra), packed_rows(rb)
    x, y, z = here()
    sum_y = total_of(from_y)
    m_a, m_c = sum_y[:ra], sum_y[ra : ra + rc]
    gram_ba, gram_bc = sum_y[ra + rc : ra + rc + pa], sum_y[ra + rc + pa :]
    gram_ca, gram_ac = kept[:pa, :], kept[pa + 2 * pb :, :]
    grad_a[...] = scaled(gram_ba, gram_ca, ra, a_ref, (y * nz + z) * ra) - m_a
    grad_c[...] = scaled(gram_ac, gram_bc, rc, c_ref, (x * ny + y) * rc) - m_c


def swap(value, axis, distance):
    return lax.ppermute(value, axis, [(i, i ^ distance) for i in range(lax.axis_size(axis))])


def partners(values, axis, stride=1):
    count = lax.axis_size(axis) // stride
    if not isinstance(values, (list, tuple)):
        values = [values] * count
    return [values[0]] + [swap(values[s], axis, s * stride) for s in range(1, count)]


def swapped(value):
    return swap(value, "gz", 1)


def body(tensor, factor_a, factor_b, factor_c):
    nx, ny, nz = (lax.axis_size(name) for name in ("gx", "gy", "gz"))
    ra, rb, rc = factor_a.shape[0], factor_b.shape[0], factor_c.shape[0]
    pa, pb, pc = packed_rows(ra), packed_rows(rb), packed_rows(rc)
    lanes = factor_a.shape[1]
    total = ra * ny * nz
    sizes = (nx, ny, nz, ra, rb, rc)
    message = ny * ra + nx * rb + pa + pb
    f32, bf16 = jnp.float32, jnp.bfloat16
    vmem = pl.BlockSpec(memory_space=pltpu.VMEM)
    tensor = pltpu.with_memory_space_constraint(tensor, pltpu.VMEM)
    flops = 2 * 3 * tensor.size * total

    def rows(count):
        return jax.ShapeDtypeStruct((count, lanes), f32)

    def call(kernel, outs, args, scratch=(), limit=4, cost=None, space=pltpu.VMEM):
        return pl.pallas_call(
            lambda *refs: kernel(sizes, *refs),
            out_shape=outs,
            in_specs=[pl.BlockSpec(memory_space=space)] * len(args),
            out_specs=[vmem] * len(outs),
            scratch_shapes=scratch,
            compiler_params=pltpu.CompilerParams(vmem_limit_bytes=limit * MIB),
            cost_estimate=cost,
            name=kernel.__name__,
        )(*args)

    work = pl.CostEstimate(flops=flops, bytes_accessed=4 * tensor.size, transcendentals=0)

    ni, nj, nk = tensor.shape
    half = total // 2
    results = [pltpu.VMEM((GROUP * nj, half), f32)] * BUFFERS
    weight = pltpu.VMEM((2 * lanes, 2 * half), bf16)
    halves = pltpu.VMEM((2, lanes, half), f32)
    later = ni // 2

    def own_part(count):
        return pltpu.VMEM((count * nj, half), f32)

    def slices(count):
        return pltpu.VMEM((count, nk, 2 * nj), bf16)

    def gram_blocks(count):
        return pltpu.VMEM((total // count, packed_rows(count), PAIR), f32)

    def array(ref):
        return jax.ShapeDtypeStruct(ref.shape, ref.dtype)

    own_ac, own_b = call(
        own_kernel,
        [rows(ra + rc), rows(rb)],
        [pltpu.with_memory_space_constraint(value, pltpu.HBM) for value in (factor_a, factor_b, factor_c)],
        [pltpu.SemaphoreType.DMA((3,))],
        cost=work,
        space=pltpu.HBM,
    )
    ac = partners(own_ac, "gy")
    b = partners(own_b, "gx")
    pairs, turned_0, rows_b = call(
        tensor_kernel, [slices(ni), slices(ni // 2), rows(nx * rb)], [*b, tensor], (), 8, work
    )
    for_z, for_x = call(pack_kernel, [rows(ny * ra + nx * rb), rows(ny * rc)], [*ac, rows_b])
    from_x = partners(for_x, "gx")
    by_x = partners(for_z, "gz", 2)
    own_y_0, turned_1, own_c, weights_c = call(
        early_kernel,
        [own_part(ni - later), slices((ni - later) // 2), rows(half), array(weight)],
        [*from_x[: nx // 2], pairs],
        (),
        8,
        work,
    )
    (stack,) = call(stack_kernel, [rows(nz // 2 * (ny * ra + nx * rb))], [*by_x, own_c])
    from_z = [stack, swapped(stack)]
    own_y_1, turned_2 = call(later_kernel, [own_part(later), slices(later // 2)], [pairs, weights_c], (), 8, work)
    turned = [turned_0, turned_1, turned_2]
    own_core, other_core, block_a, columns_a, block_b, block_c = call(
        first_kernel,
        [rows(nz // 2 * message)] * 2 + [rows(total), array(halves), rows(total), rows(total)],
        [*from_z, *from_x[nx // 2 :], own_y_0, own_y_1, own_c, pairs],
        [
            halves, weight, halves, halves, gram_blocks(ra), gram_blocks(rb),
            *results, pltpu.VMEM((2, total, lanes), f32),
        ],
        12,
        work,
    )
    other_core = swapped(other_core)
    outs = call(
        partner_kernel,
        [rows(ny * rc + pb + pc)] * (nx // 2)
        + [rows(ny * (pa + pc)), array(gram_blocks(rb)), array(gram_blocks(rc))],
        [*turned, block_a, columns_a, block_b],
        [
            weight, pltpu.VMEM((nk, half), f32), gram_blocks(ra), gram_blocks(rc),
            *results, pltpu.VMEM((half, lanes), f32),
        ],
        8,
        work,
    )
    sums_x, (grams_b, grams_ab, grams_ac) = outs[: nx // 2], outs[nx // 2 :]
    sums_x = [swap(value, "gx", s + nx // 2) for s, value in enumerate(sums_x)]
    sums_z = call(core_kernel, [rows(message)] * (nz // 2), [own_core, other_core])
    sums_z = partners(sums_z, "gz", 2)
    own_x = call(
        own_third_kernel,
        [rows(ny * rc + pb + pc)] * (nx // 2),
        [*turned, columns_a, block_b, grams_ab, grams_ac],
        [weight, pltpu.VMEM((nk, half), f32), *results, pltpu.VMEM((half, lanes), f32)],
        8,
        work,
    )
    sums_x = [swap(value, "gx", s) if s else value for s, value in enumerate(own_x)] + sums_x
    outs = call(
        middle_kernel,
        [rows(ra + rc + pa + pc)] * ny + [rows(rb)] * nx + [rows(pa + pb + pb + pc)],
        [*sums_z, *sums_x, grams_b],
    )
    sums_y, sums_x, kept = outs[:ny], outs[ny : ny + nx], outs[ny + nx]
    sums_y = partners(sums_y, "gy")
    sums_x = partners(sums_x, "gx")
    (grad_b,) = call(grad_b_kernel, [rows(rb)], [*sums_x, kept, block_b], cost=work)
    grad_a, grad_c = call(last_kernel, [rows(ra), rows(rc)], [*sums_y[::-1], kept, block_a, block_c])
    return grad_a, grad_b, grad_c


def solution(mesh):
    in_specs = (
        P("gx", "gy", "gz"),
        P(("gy", "gz"), "gx"),
        P(("gx", "gz"), "gy"),
        P(("gx", "gy"), "gz"),
    )
    out_specs = (P(("gy", "gz"), "gx"), P(("gx", "gz"), "gy"), P(("gx", "gy"), "gz"))
    return jax.shard_map(body, mesh=mesh, in_specs=in_specs, out_specs=out_specs, check_vma=False)
```

profile of v0, /device:TPU:0, one launch (start us, length us, event | category | flops | bytes accessed | tf_op | source)
XLA Modules:
  0.0 41.0 jit_solution(5650019867194509125)
XLA Ops:
  0.6 0.9 %own_kernel.1 = (f32[48,128]{1,0:T(8,128)S(1)}, f32[32,128]{1,0:T(8,128)S(1)}) custom-call(f32[16,128]{1,0:T(8,128)} %refs_0_.1, f32[32,128]{1,0:T(8,128)} %refs_1_.1, f32[32,128]{1,0:T(8,128)} %refs_2_.2), custom_call_target="tpu_custom_call" | custom-call | flops 3221225472 | bytes 8388608 | tf_op jit(solution)/shard_map/own_kernel/pallas_call | solution.py:460
  1.6 3.0 %collective-permute-start.3 = (f32[32,128]{1,0:T(8,128)S(1)}, f32[32,128]{1,0:T(8,128)S(1)}, u32[]{:S(2)}, u32[]{:S(2)}) collective-permute-start(f32[32,128]{1,0:T(8,128)S(1)} %get-tuple-element.38.refs_0_), channel_id=1, source_target_pairs={{0,16},{16,0},{1,17},{17,1},{2,18},{18,2},{3,19},{19,3},{4,20},{20... | collective-permute-start | bytes 49160 | tf_op jit(solution)/shard_map/ppermute | solution.py:429
  4.6 3.6 %collective-permute-start.2 = (f32[48,128]{1,0:T(8,128)S(1)}, f32[48,128]{1,0:T(8,128)S(1)}, u32[]{:S(2)}, u32[]{:S(2)}) collective-permute-start(f32[48,128]{1,0:T(8,128)S(1)} %get-tuple-element.37.refs_0_), channel_id=1, source_target_pairs={{0,12},{4,8},{8,4},{12,0},{1,13},{5,9},{9,5},{13,1},{2,14},{6,10},... | collective-permute-start | bytes 73736 | tf_op jit(solution)/shard_map/ppermute | solution.py:429
  8.2 0.8 %collective-permute-start = (f32[48,128]{1,0:T(8,128)S(1)}, f32[48,128]{1,0:T(8,128)S(1)}, u32[]{:S(2)}, u32[]{:S(2)}) collective-permute-start(f32[48,128]{1,0:T(8,128)S(1)} %get-tuple-element.37.refs_0_), channel_id=1, source_target_pairs={{0,4},{4,0},{8,12},{12,8},{1,5},{5,1},{9,13},{13,9},{2,6},{6,2},{1... | collective-permute-start | bytes 73736 | tf_op jit(solution)/shard_map/ppermute | solution.py:429
  9.0 0.0 collective-permute-done.3.refs_1_
  9.0 2.3 %tensor_kernel.1 = (bf16[128,128,256]{2,1,0:T(8,128)(2,1)S(1)}, bf16[64,128,256]{2,1,0:T(8,128)(2,1)S(1)}, f32[64,128]{1,0:T(8,128)S(1)}) custom-call(f32[32,128]{1,0:T(8,128)S(1)} %get-tuple-element.38.refs_0_, f32[32,128]{1,0:T(8,128)S(1)} %collective-permute-done.3.refs_1_, f32[128,128,128]{2,1,0:T(8,128)S(1)} %copy-done), custom_call_target="tpu_custom_call" | custom-call | flops 3221225472 | bytes 8388608 | tf_op jit(solution)/shard_map/tensor_kernel/pallas_call | solution.py:460
  11.3 1.6 %collective-permute-done.1.refs_2_ = f32[48,128]{1,0:T(8,128)S(1)} collective-permute-done((f32[48,128]{1,0:T(8,128)S(1)}, f32[48,128]{1,0:T(8,128)S(1)}, u32[]{:S(2)}, u32[]{:S(2)}) %collective-permute-start.1) | collective-permute-done | bytes 24608 | tf_op jit(solution)/shard_map/ppermute | solution.py:429
  13.0 1.6 %collective-permute-start.4 = (f32[128,128]{1,0:T(8,128)S(1)}, f32[128,128]{1,0:T(8,128)S(1)}, u32[]{:S(2)}, u32[]{:S(2)}) collective-permute-start(f32[128,128]{1,0:T(8,128)S(1)} %get-tuple-element.40.refs_0_), channel_id=1, source_target_pairs={{0,2},{1,3},{2,0},{3,1},{4,6},{5,7},{6,4},{7,5},{8,10},{9,11},{10,... | collective-permute-start | bytes 196616 | tf_op jit(solution)/shard_map/ppermute | solution.py:429
  14.5 0.5 %collective-permute-start.6 = (f32[128,128]{1,0:T(8,128)S(1)}, f32[128,128]{1,0:T(8,128)S(1)}, u32[]{:S(2)}, u32[]{:S(2)}) collective-permute-start(f32[128,128]{1,0:T(8,128)S(1)} %get-tuple-element.41.refs_0_), channel_id=1, source_target_pairs={{0,16},{16,0},{1,17},{17,1},{2,18},{18,2},{3,19},{19,3},{4,20},{20... | collective-permute-start | bytes 196616 | tf_op jit(solution)/shard_map/ppermute | solution.py:429
  15.0 1.4 %early_kernel.1 = (f32[8192,128]{1,0:T(8,128)S(1)}, bf16[32,128,256]{2,1,0:T(8,128)(2,1)S(1)}, f32[128,128]{1,0:T(8,128)S(1)}, bf16[256,256]{1,0:T(8,128)(2,1)S(1)}) custom-call(f32[128,128]{1,0:T(8,128)S(1)} %get-tuple-element.41.refs_0_, bf16[128,128,256]{2,1,0:T(8,128)(2,1)S(1)} %get-tuple-element.42.refs_1_.refs_0_.refs_6_), custom_call_target="tpu_custom_call" | custom-call | flops 3221225472 | bytes 8388608 | tf_op jit(solution)/shard_map/early_kernel/pallas_call | solution.py:460
  16.4 0.9 %collective-permute-done.4.refs_1_ = f32[128,128]{1,0:T(8,128)S(1)} collective-permute-done((f32[128,128]{1,0:T(8,128)S(1)}, f32[128,128]{1,0:T(8,128)S(1)}, u32[]{:S(2)}, u32[]{:S(2)}) %collective-permute-start.4) | collective-permute-done | bytes 65568 | tf_op jit(solution)/shard_map/ppermute | solution.py:429
  17.3 0.1 collective-permute-start.5
  17.4 1.3 %later_kernel.1 = (f32[8192,128]{1,0:T(8,128)S(1)}, bf16[32,128,256]{2,1,0:T(8,128)(2,1)S(1)}) custom-call(bf16[128,128,256]{2,1,0:T(8,128)(2,1)S(1)} %get-tuple-element.42.refs_1_.refs_0_.refs_6_, bf16[256,256]{1,0:T(8,128)(2,1)S(1)} %get-tuple-element.45.refs_1_), custom_call_target="tpu_custom_call" | custom-call | flops 3221225472 | bytes 8388608 | tf_op jit(solution)/shard_map/later_kernel/pallas_call | solution.py:460
  18.6 0.1 collective-permute-done.6.refs_2_
  18.8 0.0 collective-permute-done.5.refs_1_
  18.8 4.0 %first_kernel.1 = (f32[304,128]{1,0:T(8,128)S(1)}, f32[304,128]{1,0:T(8,128)S(1)}, f32[256,128]{1,0:T(8,128)S(1)}, f32[2,128,128]{2,1,0:T(8,128)S(1)}, f32[256,128]{1,0:T(8,128)S(1)}, /*index=5*/f32[256,128]{1,0:T(8,128)S(1)}) custom-call(f32[256,128]{1,0:T(8,128)S(1)} %stack_kernel.1.refs_0_, f32[256,128]{1,0:T(8,128)S(1)} %collective-permute-done.5.refs_1_, ...), custom_call_target="tpu_custom_call" | custom-call | flops 3221225472 | bytes 8388608 | tf_op jit(solution)/shard_map/first_kernel/pallas_call | solution.py:460
  22.7 0.4 %collective-permute-start.7 = (f32[304,128]{1,0:T(8,128)S(1)}, f32[304,128]{1,0:T(8,128)S(1)}, u32[]{:S(2)}, u32[]{:S(2)}) collective-permute-start(f32[304,128]{1,0:T(8,128)S(1)} %get-tuple-element.48), channel_id=1, source_target_pairs={{0,1},{1,0},{2,3},{3,2},{4,5},{5,4},{6,7},{7,6},{8,9},{9,8},{10,11... | collective-permute-start | bytes 466952 | tf_op jit(solution)/shard_map/ppermute | solution.py:429
  23.2 3.0 %partner_kernel.1 = (f32[160,128]{1,0:T(8,128)S(1)}, f32[96,128]{1,0:T(8,128)S(1)}, f32[8,16,128]{2,1,0:T(8,128)S(1)}, f32[8,16,128]{2,1,0:T(8,128)S(1)}) custom-call(bf16[64,128,256]{2,1,0:T(8,128)(2,1)S(1)} %get-tuple-element.51.refs_0_, bf16[32,128,256]{2,1,0:T(8,128)(2,1)S(1)} %get-tuple-element.52.refs_1_, ...), custom_call_target="tpu_custom_call" | custom-call | flops 3221225472 | bytes 8388608 | tf_op jit(solution)/shard_map/partner_kernel/pallas_call | solution.py:460
  26.2 0.7 %collective-permute-start.9 = (f32[160,128]{1,0:T(8,128)S(1)}, f32[160,128]{1,0:T(8,128)S(1)}, u32[]{:S(2)}, u32[]{:S(2)}) collective-permute-start(f32[160,128]{1,0:T(8,128)S(1)} %get-tuple-element.59), channel_id=1, source_target_pairs={{0,16},{16,0},{1,17},{17,1},{2,18},{18,2},{3,19},{19,3},{4,20},{20... | collective-permute-start | bytes 245768 | tf_op jit(solution)/shard_map/ppermute | solution.py:429
  26.9 0.0 collective-permute-done.7.refs_1_
  26.9 1.4 %collective-permute-start.8 = (f32[152,128]{1,0:T(8,128)S(1)}, f32[152,128]{1,0:T(8,128)S(1)}, u32[]{:S(2)}, u32[]{:S(2)}) collective-permute-start(f32[152,128]{1,0:T(8,128)S(1)} %get-tuple-element.50), channel_id=1, source_target_pairs={{0,2},{1,3},{2,0},{3,1},{4,6},{5,7},{6,4},{7,5},{8,10},{9,11},{10,... | collective-permute-start | bytes 233480 | tf_op jit(solution)/shard_map/ppermute | solution.py:429
  28.4 2.7 %own_third_kernel.1.refs_2_ = f32[160,128]{1,0:T(8,128)S(1)} custom-call(bf16[64,128,256]{2,1,0:T(8,128)(2,1)S(1)} %get-tuple-element.51.refs_0_, bf16[32,128,256]{2,1,0:T(8,128)(2,1)S(1)} %get-tuple-element.52.refs_1_, bf16[32,128,256]{2,1,0:T(8,128)(2,1)S(1)} %get-tuple-element.53.refs_2_, f32[2,128,128]{2,1,0:T(8,128)S(1)} %get-tuple-element.54.refs_4_.refs_3_, ...), custom_call_target="tpu_custom_call" | custom-call | flops 3221225472 | bytes 8388608 | tf_op jit(solution)/shard_map/own_third_kernel/pallas_call | solution.py:460
  31.1 0.0 collective-permute-done.9.refs_3_
  31.1 0.3 collective-permute-done.8.refs_1_
  31.4 1.5 %collective-permute-start.13 = (f32[32,128]{1,0:T(8,128)S(1)}, f32[32,128]{1,0:T(8,128)S(1)}, u32[]{:S(2)}, u32[]{:S(2)}) collective-permute-start(f32[32,128]{1,0:T(8,128)S(1)} %get-tuple-element.69), channel_id=1, source_target_pairs={{0,16},{16,0},{1,17},{17,1},{2,18},{18,2},{3,19},{19,3},{4,20},{20... | collective-permute-start | bytes 49160 | tf_op jit(solution)/shard_map/ppermute | solution.py:429
  32.9 2.0 %collective-permute-start.10 = (f32[72,128]{1,0:T(8,128)S(1)}, f32[72,128]{1,0:T(8,128)S(1)}, u32[]{:S(2)}, u32[]{:S(2)}) collective-permute-start(f32[72,128]{1,0:T(8,128)S(1)} %get-tuple-element.61), channel_id=1, source_target_pairs={{0,12},{4,8},{8,4},{12,0},{1,13},{5,9},{9,5},{13,1},{2,14},{6,10},... | collective-permute-start | bytes 110600 | tf_op jit(solution)/shard_map/ppermute | solution.py:429
  34.9 0.0 collective-permute-start.11
  34.9 2.4 %collective-permute-start.12 = (f32[72,128]{1,0:T(8,128)S(1)}, f32[72,128]{1,0:T(8,128)S(1)}, u32[]{:S(2)}, u32[]{:S(2)}) collective-permute-start(f32[72,128]{1,0:T(8,128)S(1)} %get-tuple-element.63), channel_id=1, source_target_pairs={{0,4},{4,0},{8,12},{12,8},{1,5},{5,1},{9,13},{13,9},{2,6},{6,2},{1... | collective-permute-start | bytes 110600 | tf_op jit(solution)/shard_map/ppermute | solution.py:429
  37.3 0.8 %grad_b_kernel.1 = f32[32,128]{1,0:T(8,128)} custom-call(f32[32,128]{1,0:T(8,128)S(1)} %get-tuple-element.68.refs_0_, f32[32,128]{1,0:T(8,128)S(1)} %collective-permute-done.13.refs_1_, f32[56,128]{1,0:T(8,128)S(1)} %get-tuple-element.65.refs_4_.refs_2_, f32[256,128]{1,0:T(8,128)S(1)} %get-tuple-element.55.refs_5_.refs_4_.refs_3_), custom_call_target="tpu_custom_call" | custom-call | flops 3221225472 | bytes 8388608 | tf_op jit(solution)/shard_map/grad_b_kernel/pallas_call | solution.py:460
  38.1 0.8 %collective-permute-done.10.refs_0_ = f32[72,128]{1,0:T(8,128)S(1)} collective-permute-done((f32[72,128]{1,0:T(8,128)S(1)}, f32[72,128]{1,0:T(8,128)S(1)}, u32[]{:S(2)}, u32[]{:S(2)}) %collective-permute-start.10) | collective-permute-done | bytes 36896 | tf_op jit(solution)/shard_map/ppermute | solution.py:429
  38.9 1.3 %collective-permute-done.11.refs_1_ = f32[72,128]{1,0:T(8,128)S(1)} collective-permute-done((f32[72,128]{1,0:T(8,128)S(1)}, f32[72,128]{1,0:T(8,128)S(1)}, u32[]{:S(2)}, u32[]{:S(2)}) %collective-permute-start.11) | collective-permute-done | bytes 36896 | tf_op jit(solution)/shard_map/ppermute | solution.py:429
  40.2 0.8 %last_kernel.1 = (f32[16,128]{1,0:T(8,128)}, f32[32,128]{1,0:T(8,128)}) custom-call(f32[72,128]{1,0:T(8,128)S(1)} %collective-permute-done.10.refs_0_, f32[72,128]{1,0:T(8,128)S(1)} %collective-permute-done.11.refs_1_, f32[72,128]{1,0:T(8,128)S(1)} %collective-permute-done.12.refs_2_, f32[72,128]{1,0:T(8,128)S(1)} %get-tuple-element.64.refs_3_, ...), custom_call_target="tpu_custom_call" | custom-call | tf_op jit(solution)/shard_map/last_kernel/pallas_call | solution.py:460
  (11 shorter events, 0.1 us)
Async XLA Ops:
  0.6 8.4 %copy-start = (f32[128,128,128]{2,1,0:T(8,128)S(1)}, f32[128,128,128]{2,1,0:T(8,128)}, u32[]{:S(2)}) copy-start(f32[128,128,128]{2,1,0:T(8,128)} %refs_2_.3) | copy-start | bytes 25165828
  1.6 7.4 %collective-permute-start.3 = (f32[32,128]{1,0:T(8,128)S(1)}, f32[32,128]{1,0:T(8,128)S(1)}, u32[]{:S(2)}, u32[]{:S(2)}) collective-permute-start(f32[32,128]{1,0:T(8,128)S(1)} %get-tuple-element.38.refs_0_), channel_id=1, source_target_pairs={{0,16},{16,0},{1,17},{17,1},{2,18},{18,2},{3,19},{19,3},{4,20},{20... | collective-permute-start | bytes 49160 | tf_op jit(solution)/shard_map/ppermute | solution.py:429
  4.6 6.7 %collective-permute-start.2 = (f32[48,128]{1,0:T(8,128)S(1)}, f32[48,128]{1,0:T(8,128)S(1)}, u32[]{:S(2)}, u32[]{:S(2)}) collective-permute-start(f32[48,128]{1,0:T(8,128)S(1)} %get-tuple-element.37.refs_0_), channel_id=1, source_target_pairs={{0,12},{4,8},{8,4},{12,0},{1,13},{5,9},{9,5},{13,1},{2,14},{6,10},... | collective-permute-start | bytes 73736 | tf_op jit(solution)/shard_map/ppermute | solution.py:429
  8.2 4.7 %collective-permute-start.1 = (f32[48,128]{1,0:T(8,128)S(1)}, f32[48,128]{1,0:T(8,128)S(1)}, u32[]{:S(2)}, u32[]{:S(2)}) collective-permute-start(f32[48,128]{1,0:T(8,128)S(1)} %get-tuple-element.37.refs_0_), channel_id=1, source_target_pairs={{0,8},{4,12},{8,0},{12,4},{1,9},{5,13},{9,1},{13,5},{2,10},{6,14},... | collective-permute-start | bytes 73736 | tf_op jit(solution)/shard_map/ppermute | solution.py:429
  8.2 4.7 %collective-permute-start = (f32[48,128]{1,0:T(8,128)S(1)}, f32[48,128]{1,0:T(8,128)S(1)}, u32[]{:S(2)}, u32[]{:S(2)}) collective-permute-start(f32[48,128]{1,0:T(8,128)S(1)} %get-tuple-element.37.refs_0_), channel_id=1, source_target_pairs={{0,4},{4,0},{8,12},{12,8},{1,5},{5,1},{9,13},{13,9},{2,6},{6,2},{1... | collective-permute-start | bytes 73736 | tf_op jit(solution)/shard_map/ppermute | solution.py:429
  13.0 4.3 %collective-permute-start.4 = (f32[128,128]{1,0:T(8,128)S(1)}, f32[128,128]{1,0:T(8,128)S(1)}, u32[]{:S(2)}, u32[]{:S(2)}) collective-permute-start(f32[128,128]{1,0:T(8,128)S(1)} %get-tuple-element.40.refs_0_), channel_id=1, source_target_pairs={{0,2},{1,3},{2,0},{3,1},{4,6},{5,7},{6,4},{7,5},{8,10},{9,11},{10,... | collective-permute-start | bytes 196616 | tf_op jit(solution)/shard_map/ppermute | solution.py:429
  14.5 4.3 %collective-permute-start.6 = (f32[128,128]{1,0:T(8,128)S(1)}, f32[128,128]{1,0:T(8,128)S(1)}, u32[]{:S(2)}, u32[]{:S(2)}) collective-permute-start(f32[128,128]{1,0:T(8,128)S(1)} %get-tuple-element.41.refs_0_), channel_id=1, source_target_pairs={{0,16},{16,0},{1,17},{17,1},{2,18},{18,2},{3,19},{19,3},{4,20},{20... | collective-permute-start | bytes 196616 | tf_op jit(solution)/shard_map/ppermute | solution.py:429
  17.3 1.5 %collective-permute-start.5 = (f32[256,128]{1,0:T(8,128)S(1)}, f32[256,128]{1,0:T(8,128)S(1)}, u32[]{:S(2)}, u32[]{:S(2)}) collective-permute-start(f32[256,128]{1,0:T(8,128)S(1)} %stack_kernel.1.refs_0_), channel_id=1, source_target_pairs={{0,1},{1,0},{2,3},{3,2},{4,5},{5,4},{6,7},{7,6},{8,9},{9,8},{10,11... | collective-permute-start | bytes 393224 | tf_op jit(solution)/shard_map/ppermute | solution.py:429
  22.7 4.2 %collective-permute-start.7 = (f32[304,128]{1,0:T(8,128)S(1)}, f32[304,128]{1,0:T(8,128)S(1)}, u32[]{:S(2)}, u32[]{:S(2)}) collective-permute-start(f32[304,128]{1,0:T(8,128)S(1)} %get-tuple-element.48), channel_id=1, source_target_pairs={{0,1},{1,0},{2,3},{3,2},{4,5},{5,4},{6,7},{7,6},{8,9},{9,8},{10,11... | collective-permute-start | bytes 466952 | tf_op jit(solution)/shard_map/ppermute | solution.py:429
  26.2 4.9 %collective-permute-start.9 = (f32[160,128]{1,0:T(8,128)S(1)}, f32[160,128]{1,0:T(8,128)S(1)}, u32[]{:S(2)}, u32[]{:S(2)}) collective-permute-start(f32[160,128]{1,0:T(8,128)S(1)} %get-tuple-element.59), channel_id=1, source_target_pairs={{0,16},{16,0},{1,17},{17,1},{2,18},{18,2},{3,19},{19,3},{4,20},{20... | collective-permute-start | bytes 245768 | tf_op jit(solution)/shard_map/ppermute | solution.py:429
  26.9 4.5 %collective-permute-start.8 = (f32[152,128]{1,0:T(8,128)S(1)}, f32[152,128]{1,0:T(8,128)S(1)}, u32[]{:S(2)}, u32[]{:S(2)}) collective-permute-start(f32[152,128]{1,0:T(8,128)S(1)} %get-tuple-element.50), channel_id=1, source_target_pairs={{0,2},{1,3},{2,0},{3,1},{4,6},{5,7},{6,4},{7,5},{8,10},{9,11},{10,... | collective-permute-start | bytes 233480 | tf_op jit(solution)/shard_map/ppermute | solution.py:429
  31.4 5.9 %collective-permute-start.13 = (f32[32,128]{1,0:T(8,128)S(1)}, f32[32,128]{1,0:T(8,128)S(1)}, u32[]{:S(2)}, u32[]{:S(2)}) collective-permute-start(f32[32,128]{1,0:T(8,128)S(1)} %get-tuple-element.69), channel_id=1, source_target_pairs={{0,16},{16,0},{1,17},{17,1},{2,18},{18,2},{3,19},{19,3},{4,20},{20... | collective-permute-start | bytes 49160 | tf_op jit(solution)/shard_map/ppermute | solution.py:429
  32.9 6.0 %collective-permute-start.10 = (f32[72,128]{1,0:T(8,128)S(1)}, f32[72,128]{1,0:T(8,128)S(1)}, u32[]{:S(2)}, u32[]{:S(2)}) collective-permute-start(f32[72,128]{1,0:T(8,128)S(1)} %get-tuple-element.61), channel_id=1, source_target_pairs={{0,12},{4,8},{8,4},{12,0},{1,13},{5,9},{9,5},{13,1},{2,14},{6,10},... | collective-permute-start | bytes 110600 | tf_op jit(solution)/shard_map/ppermute | solution.py:429
  34.9 5.2 %collective-permute-start.11 = (f32[72,128]{1,0:T(8,128)S(1)}, f32[72,128]{1,0:T(8,128)S(1)}, u32[]{:S(2)}, u32[]{:S(2)}) collective-permute-start(f32[72,128]{1,0:T(8,128)S(1)} %get-tuple-element.62), channel_id=1, source_target_pairs={{0,8},{4,12},{8,0},{12,4},{1,9},{5,13},{9,1},{13,5},{2,10},{6,14},... | collective-permute-start | bytes 110600 | tf_op jit(solution)/shard_map/ppermute | solution.py:429
  34.9 5.2 %collective-permute-start.12 = (f32[72,128]{1,0:T(8,128)S(1)}, f32[72,128]{1,0:T(8,128)S(1)}, u32[]{:S(2)}, u32[]{:S(2)}) collective-permute-start(f32[72,128]{1,0:T(8,128)S(1)} %get-tuple-element.63), channel_id=1, source_target_pairs={{0,4},{4,0},{8,12},{12,8},{1,5},{5,1},{9,13},{13,9},{2,6},{6,2},{1... | collective-permute-start | bytes 110600 | tf_op jit(solution)/shard_map/ppermute | solution.py:429
where the time goes:
time: 41.1 us; the launch traced here: 41 us
  starting transfers between devices  18 us (44%)
  Pallas kernels  17.3 us (42%)
  waiting for transfers between devices  4.99 us (12%)
  between operations  0.74 us (2%)
    ppermute x14, starting transfers between devices, swap(): lax.ppermute(value, axis, [(i, i ^ distance) for i in range(lax.axis_size...  18 us
    pallas_call x13, Pallas kernels, call(): pl.pallas_call(lambda *refs: kernel(sizes, *refs), out_shape=outs, in_spe...  17.3 us
    ppermute x14, waiting for transfers between devices, swap(): lax.ppermute(value, axis, [(i, i ^ distance) for i in range(lax.axis_size...  4.99 us
  transfers between devices with their start and end apart: 14, of which 6 were waited for; matrix products, arithmetic and copies ran while one was open for 0% of the time, Pallas kernels for 28%

commit v1 on v0

--- a/solution.py
+++ b/solution.py
@@ -8,7 +8,7 @@
 R = 64
 PAIR = 2 * R
 GROUP = 8
-UNROLL = 8
+UNROLL = 16
 BUFFERS = 4
 TILE = 8
 TURNS = 16

time: 41.1 us -> 40.5 us (0.985)
  Pallas kernels: 17.3 us -> 16.4 us
    pallas_call x13, Pallas kernels: 17.3 us -> 16.4 us  [call(): pl.pallas_call(lambda *refs: kernel(sizes, *refs), out_shape=outs, in_spe...]
  transfers between devices with their start and end apart: 14 -> 14, of which waited for: 6 -> 6; matrix products, arithmetic and copies ran while one was open for 0% -> 0% of each run, Pallas kernels for 28% -> 27%
where the time goes in v1:
time: 40.5 us; the launch traced here: 40.4 us
  starting transfers between devices  18 us (44%)
  Pallas kernels  16.4 us (40%)
  waiting for transfers between devices  5.2 us (13%)
  between operations  0.73 us (2%)
    ppermute x14, starting transfers between devices, swap(): lax.ppermute(value, axis, [(i, i ^ distance) for i in range(lax.axis_size...  18 us
    pallas_call x13, Pallas kernels, call(): pl.pallas_call(lambda *refs: kernel(sizes, *refs), out_shape=outs, in_spe...  16.4 us
    ppermute x14, waiting for transfers between devices, swap(): lax.ppermute(value, axis, [(i, i ^ distance) for i in range(lax.axis_size...  5.2 us
  transfers between devices with their start and end apart: 14, of which 6 were waited for; matrix products, arithmetic and copies ran while one was open for 0% of the time, Pallas kernels for 27%

profile of v1, /device:TPU:0, one launch (start us, length us, event | category | flops | bytes accessed | tf_op | source)
XLA Modules:
  0.0 40.4 jit_solution(12221993840536254088)
XLA Ops:
  0.6 0.9 %own_kernel.1 = (f32[48,128]{1,0:T(8,128)S(1)}, f32[32,128]{1,0:T(8,128)S(1)}) custom-call(f32[16,128]{1,0:T(8,128)} %refs_0_.1, f32[32,128]{1,0:T(8,128)} %refs_1_.1, f32[32,128]{1,0:T(8,128)} %refs_2_.2), custom_call_target="tpu_custom_call" | custom-call | flops 3221225472 | bytes 8388608 | tf_op jit(solution)/shard_map/own_kernel/pallas_call | solution.py:460
  1.6 3.0 %collective-permute-start.3 = (f32[32,128]{1,0:T(8,128)S(1)}, f32[32,128]{1,0:T(8,128)S(1)}, u32[]{:S(2)}, u32[]{:S(2)}) collective-permute-start(f32[32,128]{1,0:T(8,128)S(1)} %get-tuple-element.38.refs_0_), channel_id=1, source_target_pairs={{0,16},{16,0},{1,17},{17,1},{2,18},{18,2},{3,19},{19,3},{4,20},{20... | collective-permute-start | bytes 49160 | tf_op jit(solution)/shard_map/ppermute | solution.py:429
  4.6 3.6 %collective-permute-start.2 = (f32[48,128]{1,0:T(8,128)S(1)}, f32[48,128]{1,0:T(8,128)S(1)}, u32[]{:S(2)}, u32[]{:S(2)}) collective-permute-start(f32[48,128]{1,0:T(8,128)S(1)} %get-tuple-element.37.refs_0_), channel_id=1, source_target_pairs={{0,12},{4,8},{8,4},{12,0},{1,13},{5,9},{9,5},{13,1},{2,14},{6,10},... | collective-permute-start | bytes 73736 | tf_op jit(solution)/shard_map/ppermute | solution.py:429
  8.2 0.0 collective-permute-start.1
  8.2 0.8 %collective-permute-start = (f32[48,128]{1,0:T(8,128)S(1)}, f32[48,128]{1,0:T(8,128)S(1)}, u32[]{:S(2)}, u32[]{:S(2)}) collective-permute-start(f32[48,128]{1,0:T(8,128)S(1)} %get-tuple-element.37.refs_0_), channel_id=1, source_target_pairs={{0,4},{4,0},{8,12},{12,8},{1,5},{5,1},{9,13},{13,9},{2,6},{6,2},{1... | collective-permute-start | bytes 73736 | tf_op jit(solution)/shard_map/ppermute | solution.py:429
  9.0 0.0 collective-permute-done.3.refs_1_
  9.0 2.3 %tensor_kernel.1 = (bf16[128,128,256]{2,1,0:T(8,128)(2,1)S(1)}, bf16[64,128,256]{2,1,0:T(8,128)(2,1)S(1)}, f32[64,128]{1,0:T(8,128)S(1)}) custom-call(f32[32,128]{1,0:T(8,128)S(1)} %get-tuple-element.38.refs_0_, f32[32,128]{1,0:T(8,128)S(1)} %collective-permute-done.3.refs_1_, f32[128,128,128]{2,1,0:T(8,128)S(1)} %copy-done), custom_call_target="tpu_custom_call" | custom-call | flops 3221225472 | bytes 8388608 | tf_op jit(solution)/shard_map/tensor_kernel/pallas_call | solution.py:460
  11.3 0.0 collective-permute-done.2.refs_3_
  11.3 1.6 %collective-permute-done.1.refs_2_ = f32[48,128]{1,0:T(8,128)S(1)} collective-permute-done((f32[48,128]{1,0:T(8,128)S(1)}, f32[48,128]{1,0:T(8,128)S(1)}, u32[]{:S(2)}, u32[]{:S(2)}) %collective-permute-start.1) | collective-permute-done | bytes 24608 | tf_op jit(solution)/shard_map/ppermute | solution.py:429
  13.0 1.6 %collective-permute-start.4 = (f32[128,128]{1,0:T(8,128)S(1)}, f32[128,128]{1,0:T(8,128)S(1)}, u32[]{:S(2)}, u32[]{:S(2)}) collective-permute-start(f32[128,128]{1,0:T(8,128)S(1)} %get-tuple-element.40.refs_0_), channel_id=1, source_target_pairs={{0,2},{1,3},{2,0},{3,1},{4,6},{5,7},{6,4},{7,5},{8,10},{9,11},{10,... | collective-permute-start | bytes 196616 | tf_op jit(solution)/shard_map/ppermute | solution.py:429
  14.5 0.5 %collective-permute-start.6 = (f32[128,128]{1,0:T(8,128)S(1)}, f32[128,128]{1,0:T(8,128)S(1)}, u32[]{:S(2)}, u32[]{:S(2)}) collective-permute-start(f32[128,128]{1,0:T(8,128)S(1)} %get-tuple-element.41.refs_0_), channel_id=1, source_target_pairs={{0,16},{16,0},{1,17},{17,1},{2,18},{18,2},{3,19},{19,3},{4,20},{20... | collective-permute-start | bytes 196616 | tf_op jit(solution)/shard_map/ppermute | solution.py:429
  15.0 1.4 %early_kernel.1 = (f32[8192,128]{1,0:T(8,128)S(1)}, bf16[32,128,256]{2,1,0:T(8,128)(2,1)S(1)}, f32[128,128]{1,0:T(8,128)S(1)}, bf16[256,256]{1,0:T(8,128)(2,1)S(1)}) custom-call(f32[128,128]{1,0:T(8,128)S(1)} %get-tuple-element.41.refs_0_, bf16[128,128,256]{2,1,0:T(8,128)(2,1)S(1)} %get-tuple-element.42.refs_1_.refs_0_.refs_6_), custom_call_target="tpu_custom_call" | custom-call | flops 3221225472 | bytes 8388608 | tf_op jit(solution)/shard_map/early_kernel/pallas_call | solution.py:460
  16.4 0.9 %collective-permute-done.4.refs_1_ = f32[128,128]{1,0:T(8,128)S(1)} collective-permute-done((f32[128,128]{1,0:T(8,128)S(1)}, f32[128,128]{1,0:T(8,128)S(1)}, u32[]{:S(2)}, u32[]{:S(2)}) %collective-permute-start.4) | collective-permute-done | bytes 65568 | tf_op jit(solution)/shard_map/ppermute | solution.py:429
  17.3 0.1 collective-permute-start.5
  17.4 1.3 %later_kernel.1 = (f32[8192,128]{1,0:T(8,128)S(1)}, bf16[32,128,256]{2,1,0:T(8,128)(2,1)S(1)}) custom-call(bf16[128,128,256]{2,1,0:T(8,128)(2,1)S(1)} %get-tuple-element.42.refs_1_.refs_0_.refs_6_, bf16[256,256]{1,0:T(8,128)(2,1)S(1)} %get-tuple-element.45.refs_1_), custom_call_target="tpu_custom_call" | custom-call | flops 3221225472 | bytes 8388608 | tf_op jit(solution)/shard_map/later_kernel/pallas_call | solution.py:460
  18.6 0.1 collective-permute-done.6.refs_2_
  18.8 0.0 collective-permute-done.5.refs_1_
  18.8 3.8 %first_kernel.1 = (f32[304,128]{1,0:T(8,128)S(1)}, f32[304,128]{1,0:T(8,128)S(1)}, f32[256,128]{1,0:T(8,128)S(1)}, f32[2,128,128]{2,1,0:T(8,128)S(1)}, f32[256,128]{1,0:T(8,128)S(1)}, /*index=5*/f32[256,128]{1,0:T(8,128)S(1)}) custom-call(f32[256,128]{1,0:T(8,128)S(1)} %stack_kernel.1.refs_0_, f32[256,128]{1,0:T(8,128)S(1)} %collective-permute-done.5.refs_1_, ...), custom_call_target="tpu_custom_call" | custom-call | flops 3221225472 | bytes 8388608 | tf_op jit(solution)/shard_map/first_kernel/pallas_call | solution.py:460
  22.6 0.4 %collective-permute-start.7 = (f32[304,128]{1,0:T(8,128)S(1)}, f32[304,128]{1,0:T(8,128)S(1)}, u32[]{:S(2)}, u32[]{:S(2)}) collective-permute-start(f32[304,128]{1,0:T(8,128)S(1)} %get-tuple-element.48), channel_id=1, source_target_pairs={{0,1},{1,0},{2,3},{3,2},{4,5},{5,4},{6,7},{7,6},{8,9},{9,8},{10,11... | collective-permute-start | bytes 466952 | tf_op jit(solution)/shard_map/ppermute | solution.py:429
  23.0 2.6 %partner_kernel.1 = (f32[160,128]{1,0:T(8,128)S(1)}, f32[96,128]{1,0:T(8,128)S(1)}, f32[8,16,128]{2,1,0:T(8,128)S(1)}, f32[8,16,128]{2,1,0:T(8,128)S(1)}) custom-call(bf16[64,128,256]{2,1,0:T(8,128)(2,1)S(1)} %get-tuple-element.51.refs_0_, bf16[32,128,256]{2,1,0:T(8,128)(2,1)S(1)} %get-tuple-element.52.refs_1_, ...), custom_call_target="tpu_custom_call" | custom-call | flops 3221225472 | bytes 8388608 | tf_op jit(solution)/shard_map/partner_kernel/pallas_call | solution.py:460
  25.6 0.7 %collective-permute-start.9 = (f32[160,128]{1,0:T(8,128)S(1)}, f32[160,128]{1,0:T(8,128)S(1)}, u32[]{:S(2)}, u32[]{:S(2)}) collective-permute-start(f32[160,128]{1,0:T(8,128)S(1)} %get-tuple-element.59), channel_id=1, source_target_pairs={{0,16},{16,0},{1,17},{17,1},{2,18},{18,2},{3,19},{19,3},{4,20},{20... | collective-permute-start | bytes 245768 | tf_op jit(solution)/shard_map/ppermute | solution.py:429
  26.3 1.4 %collective-permute-start.8 = (f32[152,128]{1,0:T(8,128)S(1)}, f32[152,128]{1,0:T(8,128)S(1)}, u32[]{:S(2)}, u32[]{:S(2)}) collective-permute-start(f32[152,128]{1,0:T(8,128)S(1)} %get-tuple-element.50), channel_id=1, source_target_pairs={{0,2},{1,3},{2,0},{3,1},{4,6},{5,7},{6,4},{7,5},{8,10},{9,11},{10,... | collective-permute-start | bytes 233480 | tf_op jit(solution)/shard_map/ppermute | solution.py:429
  27.8 2.5 %own_third_kernel.1.refs_2_ = f32[160,128]{1,0:T(8,128)S(1)} custom-call(bf16[64,128,256]{2,1,0:T(8,128)(2,1)S(1)} %get-tuple-element.51.refs_0_, bf16[32,128,256]{2,1,0:T(8,128)(2,1)S(1)} %get-tuple-element.52.refs_1_, bf16[32,128,256]{2,1,0:T(8,128)(2,1)S(1)} %get-tuple-element.53.refs_2_, f32[2,128,128]{2,1,0:T(8,128)S(1)} %get-tuple-element.54.refs_4_.refs_3_, ...), custom_call_target="tpu_custom_call" | custom-call | flops 3221225472 | bytes 8388608 | tf_op jit(solution)/shard_map/own_third_kernel/pallas_call | solution.py:460
  30.3 0.0 collective-permute-done.9.refs_3_
  30.3 0.5 %collective-permute-done.8.refs_1_ = f32[152,128]{1,0:T(8,128)S(1)} collective-permute-done((f32[152,128]{1,0:T(8,128)S(1)}, f32[152,128]{1,0:T(8,128)S(1)}, u32[]{:S(2)}, u32[]{:S(2)}) %collective-permute-start.8) | collective-permute-done | bytes 77856 | tf_op jit(solution)/shard_map/ppermute | solution.py:429
  30.8 1.5 %collective-permute-start.13 = (f32[32,128]{1,0:T(8,128)S(1)}, f32[32,128]{1,0:T(8,128)S(1)}, u32[]{:S(2)}, u32[]{:S(2)}) collective-permute-start(f32[32,128]{1,0:T(8,128)S(1)} %get-tuple-element.69), channel_id=1, source_target_pairs={{0,16},{16,0},{1,17},{17,1},{2,18},{18,2},{3,19},{19,3},{4,20},{20... | collective-permute-start | bytes 49160 | tf_op jit(solution)/shard_map/ppermute | solution.py:429
  32.3 2.0 %collective-permute-start.10 = (f32[72,128]{1,0:T(8,128)S(1)}, f32[72,128]{1,0:T(8,128)S(1)}, u32[]{:S(2)}, u32[]{:S(2)}) collective-permute-start(f32[72,128]{1,0:T(8,128)S(1)} %get-tuple-element.61), channel_id=1, source_target_pairs={{0,12},{4,8},{8,4},{12,0},{1,13},{5,9},{9,5},{13,1},{2,14},{6,10},... | collective-permute-start | bytes 110600 | tf_op jit(solution)/shard_map/ppermute | solution.py:429
  34.3 2.4 %collective-permute-start.12 = (f32[72,128]{1,0:T(8,128)S(1)}, f32[72,128]{1,0:T(8,128)S(1)}, u32[]{:S(2)}, u32[]{:S(2)}) collective-permute-start(f32[72,128]{1,0:T(8,128)S(1)} %get-tuple-element.63), channel_id=1, source_target_pairs={{0,4},{4,0},{8,12},{12,8},{1,5},{5,1},{9,13},{13,9},{2,6},{6,2},{1... | collective-permute-start | bytes 110600 | tf_op jit(solution)/shard_map/ppermute | solution.py:429
  36.7 0.8 %grad_b_kernel.1 = f32[32,128]{1,0:T(8,128)} custom-call(f32[32,128]{1,0:T(8,128)S(1)} %get-tuple-element.68.refs_0_, f32[32,128]{1,0:T(8,128)S(1)} %collective-permute-done.13.refs_1_, f32[56,128]{1,0:T(8,128)S(1)} %get-tuple-element.65.refs_4_.refs_2_, f32[256,128]{1,0:T(8,128)S(1)} %get-tuple-element.55.refs_5_.refs_4_.refs_3_), custom_call_target="tpu_custom_call" | custom-call | flops 3221225472 | bytes 8388608 | tf_op jit(solution)/shard_map/grad_b_kernel/pallas_call | solution.py:460
  37.5 1.0 %collective-permute-done.10.refs_0_ = f32[72,128]{1,0:T(8,128)S(1)} collective-permute-done((f32[72,128]{1,0:T(8,128)S(1)}, f32[72,128]{1,0:T(8,128)S(1)}, u32[]{:S(2)}, u32[]{:S(2)}) %collective-permute-start.10) | collective-permute-done | bytes 36896 | tf_op jit(solution)/shard_map/ppermute | solution.py:429
  38.5 1.1 %collective-permute-done.11.refs_1_ = f32[72,128]{1,0:T(8,128)S(1)} collective-permute-done((f32[72,128]{1,0:T(8,128)S(1)}, f32[72,128]{1,0:T(8,128)S(1)}, u32[]{:S(2)}, u32[]{:S(2)}) %collective-permute-start.11) | collective-permute-done | bytes 36896 | tf_op jit(solution)/shard_map/ppermute | solution.py:429
  39.6 0.8 %last_kernel.1 = (f32[16,128]{1,0:T(8,128)}, f32[32,128]{1,0:T(8,128)}) custom-call(f32[72,128]{1,0:T(8,128)S(1)} %collective-permute-done.10.refs_0_, f32[72,128]{1,0:T(8,128)S(1)} %collective-permute-done.11.refs_1_, f32[72,128]{1,0:T(8,128)S(1)} %collective-permute-done.12.refs_2_, f32[72,128]{1,0:T(8,128)S(1)} %get-tuple-element.64.refs_3_, ...), custom_call_target="tpu_custom_call" | custom-call | tf_op jit(solution)/shard_map/last_kernel/pallas_call | solution.py:460
  (11 shorter events, 0.1 us)
Async XLA Ops:
  0.6 8.4 %copy-start = (f32[128,128,128]{2,1,0:T(8,128)S(1)}, f32[128,128,128]{2,1,0:T(8,128)}, u32[]{:S(2)}) copy-start(f32[128,128,128]{2,1,0:T(8,128)} %refs_2_.3) | copy-start | bytes 25165828
  1.6 7.4 %collective-permute-start.3 = (f32[32,128]{1,0:T(8,128)S(1)}, f32[32,128]{1,0:T(8,128)S(1)}, u32[]{:S(2)}, u32[]{:S(2)}) collective-permute-start(f32[32,128]{1,0:T(8,128)S(1)} %get-tuple-element.38.refs_0_), channel_id=1, source_target_pairs={{0,16},{16,0},{1,17},{17,1},{2,18},{18,2},{3,19},{19,3},{4,20},{20... | collective-permute-start | bytes 49160 | tf_op jit(solution)/shard_map/ppermute | solution.py:429
  4.6 6.7 %collective-permute-start.2 = (f32[48,128]{1,0:T(8,128)S(1)}, f32[48,128]{1,0:T(8,128)S(1)}, u32[]{:S(2)}, u32[]{:S(2)}) collective-permute-start(f32[48,128]{1,0:T(8,128)S(1)} %get-tuple-element.37.refs_0_), channel_id=1, source_target_pairs={{0,12},{4,8},{8,4},{12,0},{1,13},{5,9},{9,5},{13,1},{2,14},{6,10},... | collective-permute-start | bytes 73736 | tf_op jit(solution)/shard_map/ppermute | solution.py:429
  8.2 4.7 %collective-permute-start.1 = (f32[48,128]{1,0:T(8,128)S(1)}, f32[48,128]{1,0:T(8,128)S(1)}, u32[]{:S(2)}, u32[]{:S(2)}) collective-permute-start(f32[48,128]{1,0:T(8,128)S(1)} %get-tuple-element.37.refs_0_), channel_id=1, source_target_pairs={{0,8},{4,12},{8,0},{12,4},{1,9},{5,13},{9,1},{13,5},{2,10},{6,14},... | collective-permute-start | bytes 73736 | tf_op jit(solution)/shard_map/ppermute | solution.py:429
  8.2 4.7 %collective-permute-start = (f32[48,128]{1,0:T(8,128)S(1)}, f32[48,128]{1,0:T(8,128)S(1)}, u32[]{:S(2)}, u32[]{:S(2)}) collective-permute-start(f32[48,128]{1,0:T(8,128)S(1)} %get-tuple-element.37.refs_0_), channel_id=1, source_target_pairs={{0,4},{4,0},{8,12},{12,8},{1,5},{5,1},{9,13},{13,9},{2,6},{6,2},{1... | collective-permute-start | bytes 73736 | tf_op jit(solution)/shard_map/ppermute | solution.py:429
  13.0 4.3 %collective-permute-start.4 = (f32[128,128]{1,0:T(8,128)S(1)}, f32[128,128]{1,0:T(8,128)S(1)}, u32[]{:S(2)}, u32[]{:S(2)}) collective-permute-start(f32[128,128]{1,0:T(8,128)S(1)} %get-tuple-element.40.refs_0_), channel_id=1, source_target_pairs={{0,2},{1,3},{2,0},{3,1},{4,6},{5,7},{6,4},{7,5},{8,10},{9,11},{10,... | collective-permute-start | bytes 196616 | tf_op jit(solution)/shard_map/ppermute | solution.py:429
  14.5 4.3 %collective-permute-start.6 = (f32[128,128]{1,0:T(8,128)S(1)}, f32[128,128]{1,0:T(8,128)S(1)}, u32[]{:S(2)}, u32[]{:S(2)}) collective-permute-start(f32[128,128]{1,0:T(8,128)S(1)} %get-tuple-element.41.refs_0_), channel_id=1, source_target_pairs={{0,16},{16,0},{1,17},{17,1},{2,18},{18,2},{3,19},{19,3},{4,20},{20... | collective-permute-start | bytes 196616 | tf_op jit(solution)/shard_map/ppermute | solution.py:429
  17.3 1.5 %collective-permute-start.5 = (f32[256,128]{1,0:T(8,128)S(1)}, f32[256,128]{1,0:T(8,128)S(1)}, u32[]{:S(2)}, u32[]{:S(2)}) collective-permute-start(f32[256,128]{1,0:T(8,128)S(1)} %stack_kernel.1.refs_0_), channel_id=1, source_target_pairs={{0,1},{1,0},{2,3},{3,2},{4,5},{5,4},{6,7},{7,6},{8,9},{9,8},{10,11... | collective-permute-start | bytes 393224 | tf_op jit(solution)/shard_map/ppermute | solution.py:429
  22.6 3.7 %collective-permute-start.7 = (f32[304,128]{1,0:T(8,128)S(1)}, f32[304,128]{1,0:T(8,128)S(1)}, u32[]{:S(2)}, u32[]{:S(2)}) collective-permute-start(f32[304,128]{1,0:T(8,128)S(1)} %get-tuple-element.48), channel_id=1, source_target_pairs={{0,1},{1,0},{2,3},{3,2},{4,5},{5,4},{6,7},{7,6},{8,9},{9,8},{10,11... | collective-permute-start | bytes 466952 | tf_op jit(solution)/shard_map/ppermute | solution.py:429
  25.6 4.7 %collective-permute-start.9 = (f32[160,128]{1,0:T(8,128)S(1)}, f32[160,128]{1,0:T(8,128)S(1)}, u32[]{:S(2)}, u32[]{:S(2)}) collective-permute-start(f32[160,128]{1,0:T(8,128)S(1)} %get-tuple-element.59), channel_id=1, source_target_pairs={{0,16},{16,0},{1,17},{17,1},{2,18},{18,2},{3,19},{19,3},{4,20},{20... | collective-permute-start | bytes 245768 | tf_op jit(solution)/shard_map/ppermute | solution.py:429
  26.3 4.5 %collective-permute-start.8 = (f32[152,128]{1,0:T(8,128)S(1)}, f32[152,128]{1,0:T(8,128)S(1)}, u32[]{:S(2)}, u32[]{:S(2)}) collective-permute-start(f32[152,128]{1,0:T(8,128)S(1)} %get-tuple-element.50), channel_id=1, source_target_pairs={{0,2},{1,3},{2,0},{3,1},{4,6},{5,7},{6,4},{7,5},{8,10},{9,11},{10,... | collective-permute-start | bytes 233480 | tf_op jit(solution)/shard_map/ppermute | solution.py:429
  30.8 5.9 %collective-permute-start.13 = (f32[32,128]{1,0:T(8,128)S(1)}, f32[32,128]{1,0:T(8,128)S(1)}, u32[]{:S(2)}, u32[]{:S(2)}) collective-permute-start(f32[32,128]{1,0:T(8,128)S(1)} %get-tuple-element.69), channel_id=1, source_target_pairs={{0,16},{16,0},{1,17},{17,1},{2,18},{18,2},{3,19},{19,3},{4,20},{20... | collective-permute-start | bytes 49160 | tf_op jit(solution)/shard_map/ppermute | solution.py:429
  32.3 6.2 %collective-permute-start.10 = (f32[72,128]{1,0:T(8,128)S(1)}, f32[72,128]{1,0:T(8,128)S(1)}, u32[]{:S(2)}, u32[]{:S(2)}) collective-permute-start(f32[72,128]{1,0:T(8,128)S(1)} %get-tuple-element.61), channel_id=1, source_target_pairs={{0,12},{4,8},{8,4},{12,0},{1,13},{5,9},{9,5},{13,1},{2,14},{6,10},... | collective-permute-start | bytes 110600 | tf_op jit(solution)/shard_map/ppermute | solution.py:429
  34.3 5.2 %collective-permute-start.11 = (f32[72,128]{1,0:T(8,128)S(1)}, f32[72,128]{1,0:T(8,128)S(1)}, u32[]{:S(2)}, u32[]{:S(2)}) collective-permute-start(f32[72,128]{1,0:T(8,128)S(1)} %get-tuple-element.62), channel_id=1, source_target_pairs={{0,8},{4,12},{8,0},{12,4},{1,9},{5,13},{9,1},{13,5},{2,10},{6,14},... | collective-permute-start | bytes 110600 | tf_op jit(solution)/shard_map/ppermute | solution.py:429
  34.3 5.2 %collective-permute-start.12 = (f32[72,128]{1,0:T(8,128)S(1)}, f32[72,128]{1,0:T(8,128)S(1)}, u32[]{:S(2)}, u32[]{:S(2)}) collective-permute-start(f32[72,128]{1,0:T(8,128)S(1)} %get-tuple-element.63), channel_id=1, source_target_pairs={{0,4},{4,0},{8,12},{12,8},{1,5},{5,1},{9,13},{13,9},{2,6},{6,2},{1... | collective-permute-start | bytes 110600 | tf_op jit(solution)/shard_map/ppermute | solution.py:429

commit v2 on v1

--- a/solution.py
+++ b/solution.py
@@ -9,9 +9,9 @@
 PAIR = 2 * R
 GROUP = 8
 UNROLL = 16
-BUFFERS = 4
+BUFFERS = 8
 TILE = 8
-TURNS = 16
+TURNS = 64
 MIB = 1024 * 1024
 
 
@@ -93,17 +93,12 @@
     return total
 
 
-def own_kernel(sizes, a_ref, b_ref, c_ref, ac_ref, own_b, sems):
-    ra = a_ref.shape[0]
-    targets = [ac_ref.at[:ra], own_b, ac_ref.at[ra:]]
-    copies = [
-        pltpu.make_async_copy(source, target, sems.at[n])
-        for n, (source, target) in enumerate(zip([a_ref, b_ref, c_ref], targets))
-    ]
-    for copy in copies:
-        copy.start()
-    for copy in copies:
-        copy.wait()
+def token_kernel(sizes, token):
+    token[...] = jnp.zeros_like(token)
+
+
+def own_kernel(sizes, a_ref, c_ref, _, ac_ref):
+    put(ac_ref, [a_ref[...], c_ref[...]])
 
 
 def pack_kernel(sizes, *refs):
@@ -144,10 +139,6 @@
     value = jnp.dot(pair, weights, preferred_element_type=jnp.float32)
     half = value.shape[1] // 2
     return value[:, :half] + value[:, half:]
-
-
-def accurate(rows, columns):
-    return product(jnp.concatenate(split(rows), axis=1), weights(columns))
 
 
 def flat(block):
@@ -395,34 +386,41 @@
     put(kept, [sum_z[ny * ra + nx * rb :], sum_x[ny * rc :]])
 
 
-def scaled(one, other, rows, factor_ref, first_row):
+def scaled(one, other, rows, pair_weights, first_row):
     hessian = unpacked(one * other, rows)
     lane = lax.broadcasted_iota(jnp.int32, hessian.shape, 1)
     hessian = jnp.where(lane // R == lax.rem(first_row // R, 2), hessian, 0.0)
+    return product(jnp.concatenate(split(hessian), axis=1), pair_weights)
+
+
+def pair_weights(factor_ref, first_row):
     pair = pl.multiple_of(first_row // PAIR * PAIR, PAIR)
-    return accurate(hessian, factor_ref[pl.ds(pair, PAIR), :])
+    return weights(factor_ref[pl.ds(pair, PAIR), :])
 
 
 def grad_b_kernel(sizes, *refs):
     nx, ny, nz, ra, rb, rc = sizes
-    (from_x, (kept, b_ref, grad_b)), _ = take(refs, nx, 3)
+    (from_x, (kept, a_ref, b_ref, c_ref, grad_b, weights_a, weights_c)), _ = take(refs, nx, 7)
     pa, pb = packed_rows(ra), packed_rows(rb)
     x, y, z = here()
     gram_cb, gram_ab = kept[pa : pa + pb, :], kept[pa + pb : pa + 2 * pb, :]
-    grad_b[...] = scaled(gram_ab, gram_cb, rb, b_ref, (x * nz + z) * rb) - total_of(from_x)
+    first = (x * nz + z) * rb
+    grad_b[...] = scaled(gram_ab, gram_cb, rb, pair_weights(b_ref, first), first) - total_of(from_x)
+    weights_a[...] = pair_weights(a_ref, (y * nz + z) * ra)
+    weights_c[...] = pair_weights(c_ref, (x * ny + y) * rc)
 
 
 def last_kernel(sizes, *refs):
     nx, ny, nz, ra, rb, rc = sizes
-    (from_y, (kept, a_ref, c_ref, grad_a, grad_c)), _ = take(refs, ny, 5)
+    (from_y, (kept, weights_a, weights_c, grad_a, grad_c)), _ = take(refs, ny, 5)
     pa, pb = packed_rows(ra), packed_rows(rb)
     x, y, z = here()
     sum_y = total_of(from_y)
     m_a, m_c = sum_y[:ra], sum_y[ra : ra + rc]
     gram_ba, gram_bc = sum_y[ra + rc : ra + rc + pa], sum_y[ra + rc + pa :]
     gram_ca, gram_ac = kept[:pa, :], kept[pa + 2 * pb :, :]
-    grad_a[...] = scaled(gram_ba, gram_ca, ra, a_ref, (y * nz + z) * ra) - m_a
-    grad_c[...] = scaled(gram_ac, gram_bc, rc, c_ref, (x * ny + y) * rc) - m_c
+    grad_a[...] = scaled(gram_ba, gram_ca, ra, weights_a[...], (y * nz + z) * ra) - m_a
+    grad_c[...] = scaled(gram_ac, gram_bc, rc, weights_c[...], (x * ny + y) * rc) - m_c
 
 
 def swap(value, axis, distance):
@@ -489,16 +487,15 @@
     def array(ref):
         return jax.ShapeDtypeStruct(ref.shape, ref.dtype)
 
-    own_ac, own_b = call(
+    (token,) = call(token_kernel, [rows(TILE)], [], cost=work)
+    (own_ac,) = call(
         own_kernel,
-        [rows(ra + rc), rows(rb)],
-        [pltpu.with_memory_space_constraint(value, pltpu.HBM) for value in (factor_a, factor_b, factor_c)],
-        [pltpu.SemaphoreType.DMA((3,))],
+        [rows(ra + rc)],
+        [*(pltpu.with_memory_space_constraint(value, pltpu.VMEM) for value in (factor_a, factor_c)), token],
         cost=work,
-        space=pltpu.HBM,
     )
     ac = partners(own_ac, "gy")
-    b = partners(own_b, "gx")
+    b = partners(factor_b, "gx")
     pairs, turned_0, rows_b = call(
         tensor_kernel, [slices(ni), slices(ni // 2), rows(nx * rb)], [*b, tensor], (), 8, work
     )
@@ -562,8 +559,14 @@
     sums_y, sums_x, kept = outs[:ny], outs[ny : ny + nx], outs[ny + nx]
     sums_y = partners(sums_y, "gy")
     sums_x = partners(sums_x, "gx")
-    (grad_b,) = call(grad_b_kernel, [rows(rb)], [*sums_x, kept, block_b], cost=work)
-    grad_a, grad_c = call(last_kernel, [rows(ra), rows(rc)], [*sums_y[::-1], kept, block_a, block_c])
+    pair = pltpu.VMEM((2 * PAIR, 2 * lanes), bf16)
+    grad_b, weights_a, weights_c = call(
+        grad_b_kernel,
+        [rows(rb), array(pair), array(pair)],
+        [*sums_x, kept, block_a, block_b, block_c],
+        cost=work,
+    )
+    grad_a, grad_c = call(last_kernel, [rows(ra), rows(rc)], [*sums_y[::-1], kept, weights_a, weights_c])
     return grad_a, grad_b, grad_c
 
 

time: 40.5 us -> 39.1 us (0.965)
  Pallas kernels: 16.4 us -> 14.7 us
    pallas_call x13 -> x14, Pallas kernels: 16.4 us -> 14.7 us  [call(): pl.pallas_call(lambda *refs: kernel(sizes, *refs), out_shape=outs, in_spe...]
  transfers between devices with their start and end apart: 14 -> 14, of which waited for: 6 -> 7; matrix products, arithmetic and copies ran while one was open for 0% -> 0% of each run, Pallas kernels for 27% -> 26%
where the time goes in v2:
time: 39.1 us; the launch traced here: 38.9 us
  starting transfers between devices  18.2 us (47%)
  Pallas kernels  14.7 us (38%)
  waiting for transfers between devices  5.19 us (13%)
  between operations  0.78 us (2%)
    ppermute x14, starting transfers between devices, swap(): lax.ppermute(value, axis, [(i, i ^ distance) for i in range(lax.axis_size...  18.2 us
    pallas_call x14, Pallas kernels, call(): pl.pallas_call(lambda *refs: kernel(sizes, *refs), out_shape=outs, in_spe...  14.7 us
    ppermute x14, waiting for transfers between devices, swap(): lax.ppermute(value, axis, [(i, i ^ distance) for i in range(lax.axis_size...  5.19 us
  transfers between devices with their start and end apart: 14, of which 7 were waited for; matrix products, arithmetic and copies ran while one was open for 0% of the time, Pallas kernels for 26%

profile of v2, /device:TPU:0, one launch (start us, length us, event | category | flops | bytes accessed | tf_op | source)
XLA Modules:
  0.0 38.9 jit_solution(12678484582545276815)
XLA Ops:
  0.7 3.0 %collective-permute-start.3 = (f32[32,128]{1,0:T(8,128)}, f32[32,128]{1,0:T(8,128)S(1)}, u32[]{:S(2)}, u32[]{:S(2)}) collective-permute-start(f32[32,128]{1,0:T(8,128)} %refs_0_.3), channel_id=1, source_target_pairs={{0,16},{16,0},{1,17},{17,1},{2,18},{18,2},{3,19},{19,3},{4,20},{20... | collective-permute-start | bytes 49160 | tf_op jit(solution)/shard_map/ppermute | solution.py:427
  3.7 0.0 slice-start.1
  3.7 0.0 copy-start.1
  3.7 3.7 %collective-permute-start.2 = (f32[48,128]{1,0:T(8,128)S(1)}, f32[48,128]{1,0:T(8,128)S(1)}, u32[]{:S(2)}, u32[]{:S(2)}) collective-permute-start(f32[48,128]{1,0:T(8,128)S(1)} %own_kernel.1.refs_0_), channel_id=1, source_target_pairs={{0,12},{4,8},{8,4},{12,0},{1,13},{5,9},{9,5},{13,1},{2,14},{6,10},... | collective-permute-start | bytes 73736 | tf_op jit(solution)/shard_map/ppermute | solution.py:427
  7.4 0.8 %collective-permute-start = (f32[48,128]{1,0:T(8,128)S(1)}, f32[48,128]{1,0:T(8,128)S(1)}, u32[]{:S(2)}, u32[]{:S(2)}) collective-permute-start(f32[48,128]{1,0:T(8,128)S(1)} %own_kernel.1.refs_0_), channel_id=1, source_target_pairs={{0,4},{4,0},{8,12},{12,8},{1,5},{5,1},{9,13},{13,9},{2,6},{6,2},{1... | collective-permute-start | bytes 73736 | tf_op jit(solution)/shard_map/ppermute | solution.py:427
  8.2 1.6 %tensor_kernel.1 = (bf16[128,128,256]{2,1,0:T(8,128)(2,1)S(1)}, bf16[64,128,256]{2,1,0:T(8,128)(2,1)S(1)}, f32[64,128]{1,0:T(8,128)S(1)}) custom-call(f32[32,128]{1,0:T(8,128)S(1)} %copy-done.1, f32[32,128]{1,0:T(8,128)S(1)} %collective-permute-done.3.refs_1_, f32[128,128,128]{2,1,0:T(8,128)S(1)} %bitcast.1), custom_call_target="tpu_custom_call" | custom-call | flops 3221225472 | bytes 8388608 | tf_op jit(solution)/shard_map/tensor_kernel/pallas_call | solution.py:458
  9.8 0.0 collective-permute-done.2.refs_3_
  9.8 2.3 %collective-permute-done.1.refs_2_ = f32[48,128]{1,0:T(8,128)S(1)} collective-permute-done((f32[48,128]{1,0:T(8,128)S(1)}, f32[48,128]{1,0:T(8,128)S(1)}, u32[]{:S(2)}, u32[]{:S(2)}) %collective-permute-start.1) | collective-permute-done | bytes 24608 | tf_op jit(solution)/shard_map/ppermute | solution.py:427
  12.1 1.6 %collective-permute-start.4 = (f32[128,128]{1,0:T(8,128)S(1)}, f32[128,128]{1,0:T(8,128)S(1)}, u32[]{:S(2)}, u32[]{:S(2)}) collective-permute-start(f32[128,128]{1,0:T(8,128)S(1)} %get-tuple-element.39.refs_0_), channel_id=1, source_target_pairs={{0,2},{1,3},{2,0},{3,1},{4,6},{5,7},{6,4},{7,5},{8,10},{9,11},{10,... | collective-permute-start | bytes 196616 | tf_op jit(solution)/shard_map/ppermute | solution.py:427
  13.7 0.6 %collective-permute-start.6 = (f32[128,128]{1,0:T(8,128)S(1)}, f32[128,128]{1,0:T(8,128)S(1)}, u32[]{:S(2)}, u32[]{:S(2)}) collective-permute-start(f32[128,128]{1,0:T(8,128)S(1)} %get-tuple-element.40.refs_0_), channel_id=1, source_target_pairs={{0,16},{16,0},{1,17},{17,1},{2,18},{18,2},{3,19},{19,3},{4,20},{20... | collective-permute-start | bytes 196616 | tf_op jit(solution)/shard_map/ppermute | solution.py:427
  14.3 1.4 %early_kernel.1 = (f32[8192,128]{1,0:T(8,128)S(1)}, bf16[32,128,256]{2,1,0:T(8,128)(2,1)S(1)}, f32[128,128]{1,0:T(8,128)S(1)}, bf16[256,256]{1,0:T(8,128)(2,1)S(1)}) custom-call(f32[128,128]{1,0:T(8,128)S(1)} %get-tuple-element.40.refs_0_, bf16[128,128,256]{2,1,0:T(8,128)(2,1)S(1)} %get-tuple-element.41.refs_1_.refs_0_.refs_6_), custom_call_target="tpu_custom_call" | custom-call | flops 3221225472 | bytes 8388608 | tf_op jit(solution)/shard_map/early_kernel/pallas_call | solution.py:458
  15.7 0.8 %collective-permute-done.4.refs_1_ = f32[128,128]{1,0:T(8,128)S(1)} collective-permute-done((f32[128,128]{1,0:T(8,128)S(1)}, f32[128,128]{1,0:T(8,128)S(1)}, u32[]{:S(2)}, u32[]{:S(2)}) %collective-permute-start.4) | collective-permute-done | bytes 65568 | tf_op jit(solution)/shard_map/ppermute | solution.py:427
  16.5 0.1 collective-permute-start.5
  16.6 1.2 %later_kernel.1 = (f32[8192,128]{1,0:T(8,128)S(1)}, bf16[32,128,256]{2,1,0:T(8,128)(2,1)S(1)}) custom-call(bf16[128,128,256]{2,1,0:T(8,128)(2,1)S(1)} %get-tuple-element.41.refs_1_.refs_0_.refs_6_, bf16[256,256]{1,0:T(8,128)(2,1)S(1)} %get-tuple-element.44.refs_1_), custom_call_target="tpu_custom_call" | custom-call | flops 3221225472 | bytes 8388608 | tf_op jit(solution)/shard_map/later_kernel/pallas_call | solution.py:458
  17.8 0.1 collective-permute-done.6.refs_2_
  18.0 3.7 %first_kernel.1 = (f32[304,128]{1,0:T(8,128)S(1)}, f32[304,128]{1,0:T(8,128)S(1)}, f32[256,128]{1,0:T(8,128)S(1)}, f32[2,128,128]{2,1,0:T(8,128)S(1)}, f32[256,128]{1,0:T(8,128)S(1)}, /*index=5*/f32[256,128]{1,0:T(8,128)S(1)}) custom-call(f32[256,128]{1,0:T(8,128)S(1)} %stack_kernel.1.refs_0_, f32[256,128]{1,0:T(8,128)S(1)} %collective-permute-done.5.refs_1_, ...), custom_call_target="tpu_custom_call" | custom-call | flops 3221225472 | bytes 8388608 | tf_op jit(solution)/shard_map/first_kernel/pallas_call | solution.py:458
  21.7 0.4 %collective-permute-start.7 = (f32[304,128]{1,0:T(8,128)S(1)}, f32[304,128]{1,0:T(8,128)S(1)}, u32[]{:S(2)}, u32[]{:S(2)}) collective-permute-start(f32[304,128]{1,0:T(8,128)S(1)} %get-tuple-element.47), channel_id=1, source_target_pairs={{0,1},{1,0},{2,3},{3,2},{4,5},{5,4},{6,7},{7,6},{8,9},{9,8},{10,11... | collective-permute-start | bytes 466952 | tf_op jit(solution)/shard_map/ppermute | solution.py:427
  22.2 2.6 %partner_kernel.1 = (f32[160,128]{1,0:T(8,128)S(1)}, f32[96,128]{1,0:T(8,128)S(1)}, f32[8,16,128]{2,1,0:T(8,128)S(1)}, f32[8,16,128]{2,1,0:T(8,128)S(1)}) custom-call(bf16[64,128,256]{2,1,0:T(8,128)(2,1)S(1)} %get-tuple-element.50.refs_0_, bf16[32,128,256]{2,1,0:T(8,128)(2,1)S(1)} %get-tuple-element.51.refs_1_, ...), custom_call_target="tpu_custom_call" | custom-call | flops 3221225472 | bytes 8388608 | tf_op jit(solution)/shard_map/partner_kernel/pallas_call | solution.py:458
  24.7 0.7 %collective-permute-start.9 = (f32[160,128]{1,0:T(8,128)S(1)}, f32[160,128]{1,0:T(8,128)S(1)}, u32[]{:S(2)}, u32[]{:S(2)}) collective-permute-start(f32[160,128]{1,0:T(8,128)S(1)} %get-tuple-element.58), channel_id=1, source_target_pairs={{0,16},{16,0},{1,17},{17,1},{2,18},{18,2},{3,19},{19,3},{4,20},{20... | collective-permute-start | bytes 245768 | tf_op jit(solution)/shard_map/ppermute | solution.py:427
  25.5 1.5 %collective-permute-start.8 = (f32[152,128]{1,0:T(8,128)S(1)}, f32[152,128]{1,0:T(8,128)S(1)}, u32[]{:S(2)}, u32[]{:S(2)}) collective-permute-start(f32[152,128]{1,0:T(8,128)S(1)} %get-tuple-element.49), channel_id=1, source_target_pairs={{0,2},{1,3},{2,0},{3,1},{4,6},{5,7},{6,4},{7,5},{8,10},{9,11},{10,... | collective-permute-start | bytes 233480 | tf_op jit(solution)/shard_map/ppermute | solution.py:427
  27.0 2.5 %own_third_kernel.1.refs_2_ = f32[160,128]{1,0:T(8,128)S(1)} custom-call(bf16[64,128,256]{2,1,0:T(8,128)(2,1)S(1)} %get-tuple-element.50.refs_0_, bf16[32,128,256]{2,1,0:T(8,128)(2,1)S(1)} %get-tuple-element.51.refs_1_, bf16[32,128,256]{2,1,0:T(8,128)(2,1)S(1)} %get-tuple-element.52.refs_2_, f32[2,128,128]{2,1,0:T(8,128)S(1)} %get-tuple-element.53.refs_4_.refs_3_, ...), custom_call_target="tpu_custom_call" | custom-call | flops 3221225472 | bytes 8388608 | tf_op jit(solution)/shard_map/own_third_kernel/pallas_call | solution.py:458
  29.5 0.0 collective-permute-done.9.refs_3_
  29.5 0.4 %collective-permute-done.8.refs_1_ = f32[152,128]{1,0:T(8,128)S(1)} collective-permute-done((f32[152,128]{1,0:T(8,128)S(1)}, f32[152,128]{1,0:T(8,128)S(1)}, u32[]{:S(2)}, u32[]{:S(2)}) %collective-permute-start.8) | collective-permute-done | bytes 77856 | tf_op jit(solution)/shard_map/ppermute | solution.py:427
  30.0 1.5 %collective-permute-start.13 = (f32[32,128]{1,0:T(8,128)S(1)}, f32[32,128]{1,0:T(8,128)S(1)}, u32[]{:S(2)}, u32[]{:S(2)}) collective-permute-start(f32[32,128]{1,0:T(8,128)S(1)} %get-tuple-element.66), channel_id=1, source_target_pairs={{0,16},{16,0},{1,17},{17,1},{2,18},{18,2},{3,19},{19,3},{4,20},{20... | collective-permute-start | bytes 49160 | tf_op jit(solution)/shard_map/ppermute | solution.py:427
  31.4 1.5 %collective-permute-start.10 = (f32[72,128]{1,0:T(8,128)S(1)}, f32[72,128]{1,0:T(8,128)S(1)}, u32[]{:S(2)}, u32[]{:S(2)}) collective-permute-start(f32[72,128]{1,0:T(8,128)S(1)} %get-tuple-element.60), channel_id=1, source_target_pairs={{0,12},{4,8},{8,4},{12,0},{1,13},{5,9},{9,5},{13,1},{2,14},{6,10},... | collective-permute-start | bytes 110600 | tf_op jit(solution)/shard_map/ppermute | solution.py:427
  32.9 0.6 %collective-permute-start.11 = (f32[72,128]{1,0:T(8,128)S(1)}, f32[72,128]{1,0:T(8,128)S(1)}, u32[]{:S(2)}, u32[]{:S(2)}) collective-permute-start(f32[72,128]{1,0:T(8,128)S(1)} %get-tuple-element.61), channel_id=1, source_target_pairs={{0,8},{4,12},{8,0},{12,4},{1,9},{5,13},{9,1},{13,5},{2,10},{6,14},... | collective-permute-start | bytes 110600 | tf_op jit(solution)/shard_map/ppermute | solution.py:427
  33.4 2.4 %collective-permute-start.12 = (f32[72,128]{1,0:T(8,128)S(1)}, f32[72,128]{1,0:T(8,128)S(1)}, u32[]{:S(2)}, u32[]{:S(2)}) collective-permute-start(f32[72,128]{1,0:T(8,128)S(1)} %get-tuple-element.62), channel_id=1, source_target_pairs={{0,4},{4,0},{8,12},{12,8},{1,5},{5,1},{9,13},{13,9},{2,6},{6,2},{1... | collective-permute-start | bytes 110600 | tf_op jit(solution)/shard_map/ppermute | solution.py:427
  35.8 0.8 %grad_b_kernel.1 = (f32[32,128]{1,0:T(8,128)}, bf16[256,256]{1,0:T(8,128)(2,1)S(1)}, bf16[256,256]{1,0:T(8,128)(2,1)S(1)}) custom-call(f32[32,128]{1,0:T(8,128)S(1)} %get-tuple-element.65.refs_0_, f32[32,128]{1,0:T(8,128)S(1)} %collective-permute-done.13.refs_1_, f32[56,128]{1,0:T(8,128)S(1)} %get-tuple-element.64.refs_2_.refs_4_, ...), custom_call_target="tpu_custom_call" | custom-call | flops 3221225472 | bytes 8388608 | tf_op jit(solution)/shard_map/grad_b_kernel/pallas_call | solution.py:458
  36.6 0.6 %collective-permute-done.10.refs_0_ = f32[72,128]{1,0:T(8,128)S(1)} collective-permute-done((f32[72,128]{1,0:T(8,128)S(1)}, f32[72,128]{1,0:T(8,128)S(1)}, u32[]{:S(2)}, u32[]{:S(2)}) %collective-permute-start.10) | collective-permute-done | bytes 36896 | tf_op jit(solution)/shard_map/ppermute | solution.py:427
  37.2 0.6 %collective-permute-done.11.refs_1_ = f32[72,128]{1,0:T(8,128)S(1)} collective-permute-done((f32[72,128]{1,0:T(8,128)S(1)}, f32[72,128]{1,0:T(8,128)S(1)}, u32[]{:S(2)}, u32[]{:S(2)}) %collective-permute-start.11) | collective-permute-done | bytes 36896 | tf_op jit(solution)/shard_map/ppermute | solution.py:427
  37.8 0.4 collective-permute-done.12.refs_2_
  38.1 0.8 %last_kernel.1 = (f32[16,128]{1,0:T(8,128)}, f32[32,128]{1,0:T(8,128)}) custom-call(f32[72,128]{1,0:T(8,128)S(1)} %collective-permute-done.10.refs_0_, f32[72,128]{1,0:T(8,128)S(1)} %collective-permute-done.11.refs_1_, f32[72,128]{1,0:T(8,128)S(1)} %collective-permute-done.12.refs_2_, f32[72,128]{1,0:T(8,128)S(1)} %get-tuple-element.63.refs_3_, ...), custom_call_target="tpu_custom_call" | custom-call | tf_op jit(solution)/shard_map/last_kernel/pallas_call | solution.py:458
  (21 shorter events, 0.1 us)
Async XLA Ops:
  0.6 3.1 %copy-start = (f32[32,128]{1,0:T(8,128)S(1)}, f32[32,128]{1,0:T(8,128)}, u32[]{:S(2)}) copy-start(f32[32,128]{1,0:T(8,128)} %refs_1_.1) | copy-start | bytes 49156
  0.6 3.1 %copy-start.2 = (f32[16,128]{1,0:T(8,128)S(1)}, f32[16,128]{1,0:T(8,128)}, u32[]{:S(2)}) copy-start(f32[16,128]{1,0:T(8,128)} %refs_0_.2) | copy-start | bytes 24580
  0.7 7.5 %collective-permute-start.3 = (f32[32,128]{1,0:T(8,128)}, f32[32,128]{1,0:T(8,128)S(1)}, u32[]{:S(2)}, u32[]{:S(2)}) collective-permute-start(f32[32,128]{1,0:T(8,128)} %refs_0_.3), channel_id=1, source_target_pairs={{0,16},{16,0},{1,17},{17,1},{2,18},{18,2},{3,19},{19,3},{4,20},{20... | collective-permute-start | bytes 49160 | tf_op jit(solution)/shard_map/ppermute | solution.py:427
  3.7 4.5 %slice-start = ((s8[8388608]{0:T(1024)(128)(4,1)}), s8[4194304]{0:T(1024)(128)(4,1)S(1)}, s32[]{:S(2)}) async-start(s8[8388608]{0:T(1024)(128)(4,1)} %bitcast), calls=%async_computation | async-start | bytes 8388608
  3.7 4.5 %slice-start.1 = ((s8[8388608]{0:T(1024)(128)(4,1)}), s8[4194304]{0:T(1024)(128)(4,1)S(1)}, s32[]{:S(2)}) async-start(s8[8388608]{0:T(1024)(128)(4,1)} %bitcast), calls=%async_computation.1 | async-start | bytes 8388608
  3.7 4.5 %copy-start.1 = (f32[32,128]{1,0:T(8,128)S(1)}, f32[32,128]{1,0:T(8,128)}, u32[]{:S(2)}) copy-start(f32[32,128]{1,0:T(8,128)} %refs_0_.3) | copy-start | bytes 49156
  3.7 6.1 %collective-permute-start.2 = (f32[48,128]{1,0:T(8,128)S(1)}, f32[48,128]{1,0:T(8,128)S(1)}, u32[]{:S(2)}, u32[]{:S(2)}) collective-permute-start(f32[48,128]{1,0:T(8,128)S(1)} %own_kernel.1.refs_0_), channel_id=1, source_target_pairs={{0,12},{4,8},{8,4},{12,0},{1,13},{5,9},{9,5},{13,1},{2,14},{6,10},... | collective-permute-start | bytes 73736 | tf_op jit(solution)/shard_map/ppermute | solution.py:427
  7.4 4.7 %collective-permute-start.1 = (f32[48,128]{1,0:T(8,128)S(1)}, f32[48,128]{1,0:T(8,128)S(1)}, u32[]{:S(2)}, u32[]{:S(2)}) collective-permute-start(f32[48,128]{1,0:T(8,128)S(1)} %own_kernel.1.refs_0_), channel_id=1, source_target_pairs={{0,8},{4,12},{8,0},{12,4},{1,9},{5,13},{9,1},{13,5},{2,10},{6,14},... | collective-permute-start | bytes 73736 | tf_op jit(solution)/shard_map/ppermute | solution.py:427
  7.4 4.7 %collective-permute-start = (f32[48,128]{1,0:T(8,128)S(1)}, f32[48,128]{1,0:T(8,128)S(1)}, u32[]{:S(2)}, u32[]{:S(2)}) collective-permute-start(f32[48,128]{1,0:T(8,128)S(1)} %own_kernel.1.refs_0_), channel_id=1, source_target_pairs={{0,4},{4,0},{8,12},{12,8},{1,5},{5,1},{9,13},{13,9},{2,6},{6,2},{1... | collective-permute-start | bytes 73736 | tf_op jit(solution)/shard_map/ppermute | solution.py:427
  12.1 4.3 %collective-permute-start.4 = (f32[128,128]{1,0:T(8,128)S(1)}, f32[128,128]{1,0:T(8,128)S(1)}, u32[]{:S(2)}, u32[]{:S(2)}) collective-permute-start(f32[128,128]{1,0:T(8,128)S(1)} %get-tuple-element.39.refs_0_), channel_id=1, source_target_pairs={{0,2},{1,3},{2,0},{3,1},{4,6},{5,7},{6,4},{7,5},{8,10},{9,11},{10,... | collective-permute-start | bytes 196616 | tf_op jit(solution)/shard_map/ppermute | solution.py:427
  13.7 4.3 %collective-permute-start.6 = (f32[128,128]{1,0:T(8,128)S(1)}, f32[128,128]{1,0:T(8,128)S(1)}, u32[]{:S(2)}, u32[]{:S(2)}) collective-permute-start(f32[128,128]{1,0:T(8,128)S(1)} %get-tuple-element.40.refs_0_), channel_id=1, source_target_pairs={{0,16},{16,0},{1,17},{17,1},{2,18},{18,2},{3,19},{19,3},{4,20},{20... | collective-permute-start | bytes 196616 | tf_op jit(solution)/shard_map/ppermute | solution.py:427
  16.5 1.5 %collective-permute-start.5 = (f32[256,128]{1,0:T(8,128)S(1)}, f32[256,128]{1,0:T(8,128)S(1)}, u32[]{:S(2)}, u32[]{:S(2)}) collective-permute-start(f32[256,128]{1,0:T(8,128)S(1)} %stack_kernel.1.refs_0_), channel_id=1, source_target_pairs={{0,1},{1,0},{2,3},{3,2},{4,5},{5,4},{6,7},{7,6},{8,9},{9,8},{10,11... | collective-permute-start | bytes 393224 | tf_op jit(solution)/shard_map/ppermute | solution.py:427
  21.7 3.7 %collective-permute-start.7 = (f32[304,128]{1,0:T(8,128)S(1)}, f32[304,128]{1,0:T(8,128)S(1)}, u32[]{:S(2)}, u32[]{:S(2)}) collective-permute-start(f32[304,128]{1,0:T(8,128)S(1)} %get-tuple-element.47), channel_id=1, source_target_pairs={{0,1},{1,0},{2,3},{3,2},{4,5},{5,4},{6,7},{7,6},{8,9},{9,8},{10,11... | collective-permute-start | bytes 466952 | tf_op jit(solution)/shard_map/ppermute | solution.py:427
  24.7 4.8 %collective-permute-start.9 = (f32[160,128]{1,0:T(8,128)S(1)}, f32[160,128]{1,0:T(8,128)S(1)}, u32[]{:S(2)}, u32[]{:S(2)}) collective-permute-start(f32[160,128]{1,0:T(8,128)S(1)} %get-tuple-element.58), channel_id=1, source_target_pairs={{0,16},{16,0},{1,17},{17,1},{2,18},{18,2},{3,19},{19,3},{4,20},{20... | collective-permute-start | bytes 245768 | tf_op jit(solution)/shard_map/ppermute | solution.py:427
  25.5 4.5 %collective-permute-start.8 = (f32[152,128]{1,0:T(8,128)S(1)}, f32[152,128]{1,0:T(8,128)S(1)}, u32[]{:S(2)}, u32[]{:S(2)}) collective-permute-start(f32[152,128]{1,0:T(8,128)S(1)} %get-tuple-element.49), channel_id=1, source_target_pairs={{0,2},{1,3},{2,0},{3,1},{4,6},{5,7},{6,4},{7,5},{8,10},{9,11},{10,... | collective-permute-start | bytes 233480 | tf_op jit(solution)/shard_map/ppermute | solution.py:427
  30.0 5.9 %collective-permute-start.13 = (f32[32,128]{1,0:T(8,128)S(1)}, f32[32,128]{1,0:T(8,128)S(1)}, u32[]{:S(2)}, u32[]{:S(2)}) collective-permute-start(f32[32,128]{1,0:T(8,128)S(1)} %get-tuple-element.66), channel_id=1, source_target_pairs={{0,16},{16,0},{1,17},{17,1},{2,18},{18,2},{3,19},{19,3},{4,20},{20... | collective-permute-start | bytes 49160 | tf_op jit(solution)/shard_map/ppermute | solution.py:427
  31.4 5.8 %collective-permute-start.10 = (f32[72,128]{1,0:T(8,128)S(1)}, f32[72,128]{1,0:T(8,128)S(1)}, u32[]{:S(2)}, u32[]{:S(2)}) collective-permute-start(f32[72,128]{1,0:T(8,128)S(1)} %get-tuple-element.60), channel_id=1, source_target_pairs={{0,12},{4,8},{8,4},{12,0},{1,13},{5,9},{9,5},{13,1},{2,14},{6,10},... | collective-permute-start | bytes 110600 | tf_op jit(solution)/shard_map/ppermute | solution.py:427
  32.9 4.9 %collective-permute-start.11 = (f32[72,128]{1,0:T(8,128)S(1)}, f32[72,128]{1,0:T(8,128)S(1)}, u32[]{:S(2)}, u32[]{:S(2)}) collective-permute-start(f32[72,128]{1,0:T(8,128)S(1)} %get-tuple-element.61), channel_id=1, source_target_pairs={{0,8},{4,12},{8,0},{12,4},{1,9},{5,13},{9,1},{13,5},{2,10},{6,14},... | collective-permute-start | bytes 110600 | tf_op jit(solution)/shard_map/ppermute | solution.py:427
  33.4 4.7 %collective-permute-start.12 = (f32[72,128]{1,0:T(8,128)S(1)}, f32[72,128]{1,0:T(8,128)S(1)}, u32[]{:S(2)}, u32[]{:S(2)}) collective-permute-start(f32[72,128]{1,0:T(8,128)S(1)} %get-tuple-element.62), channel_id=1, source_target_pairs={{0,4},{4,0},{8,12},{12,8},{1,5},{5,1},{9,13},{13,9},{2,6},{6,2},{1... | collective-permute-start | bytes 110600 | tf_op jit(solution)/shard_map/ppermute | solution.py:427

commit v3 on v2

--- a/solution.py
+++ b/solution.py
@@ -7,8 +7,8 @@
 
 R = 64
 PAIR = 2 * R
-GROUP = 8
-UNROLL = 16
+GROUP = 4
+UNROLL = 32
 BUFFERS = 8
 TILE = 8
 TURNS = 64

time: 39.1 us -> 39.2 us (level)
  no operation moved by 1% of the time
where the time goes in v3:
time: 39.2 us; the launch traced here: 39 us
  starting transfers between devices  18.2 us (46%)
  Pallas kernels  14.8 us (38%)
  waiting for transfers between devices  5.21 us (13%)
  between operations  0.78 us (2%)
    ppermute x14, starting transfers between devices, swap(): lax.ppermute(value, axis, [(i, i ^ distance) for i in range(lax.axis_size...  18.2 us
    pallas_call x14, Pallas kernels, call(): pl.pallas_call(lambda *refs: kernel(sizes, *refs), out_shape=outs, in_spe...  14.8 us
    ppermute x14, waiting for transfers between devices, swap(): lax.ppermute(value, axis, [(i, i ^ distance) for i in range(lax.axis_size...  5.21 us
  transfers between devices with their start and end apart: 14, of which 7 were waited for; matrix products, arithmetic and copies ran while one was open for 0% of the time, Pallas kernels for 26%

profile of v3, /device:TPU:0, one launch (start us, length us, event | category | flops | bytes accessed | tf_op | source)
XLA Modules:
  0.0 39.0 jit_solution(12673054220716093574)
XLA Ops:
  0.7 3.0 %collective-permute-start.3 = (f32[32,128]{1,0:T(8,128)}, f32[32,128]{1,0:T(8,128)S(1)}, u32[]{:S(2)}, u32[]{:S(2)}) collective-permute-start(f32[32,128]{1,0:T(8,128)} %refs_0_.3), channel_id=1, source_target_pairs={{0,16},{16,0},{1,17},{17,1},{2,18},{18,2},{3,19},{19,3},{4,20},{20... | collective-permute-start | bytes 49160 | tf_op jit(solution)/shard_map/ppermute | solution.py:427
  3.7 0.0 slice-start.1
  3.7 0.0 copy-start.1
  3.7 3.7 %collective-permute-start.2 = (f32[48,128]{1,0:T(8,128)S(1)}, f32[48,128]{1,0:T(8,128)S(1)}, u32[]{:S(2)}, u32[]{:S(2)}) collective-permute-start(f32[48,128]{1,0:T(8,128)S(1)} %own_kernel.1.refs_0_), channel_id=1, source_target_pairs={{0,12},{4,8},{8,4},{12,0},{1,13},{5,9},{9,5},{13,1},{2,14},{6,10},... | collective-permute-start | bytes 73736 | tf_op jit(solution)/shard_map/ppermute | solution.py:427
  7.4 0.8 %collective-permute-start = (f32[48,128]{1,0:T(8,128)S(1)}, f32[48,128]{1,0:T(8,128)S(1)}, u32[]{:S(2)}, u32[]{:S(2)}) collective-permute-start(f32[48,128]{1,0:T(8,128)S(1)} %own_kernel.1.refs_0_), channel_id=1, source_target_pairs={{0,4},{4,0},{8,12},{12,8},{1,5},{5,1},{9,13},{13,9},{2,6},{6,2},{1... | collective-permute-start | bytes 73736 | tf_op jit(solution)/shard_map/ppermute | solution.py:427
  8.2 0.0 collective-permute-done.3.refs_1_
  8.2 1.6 %tensor_kernel.1 = (bf16[128,128,256]{2,1,0:T(8,128)(2,1)S(1)}, bf16[64,128,256]{2,1,0:T(8,128)(2,1)S(1)}, f32[64,128]{1,0:T(8,128)S(1)}) custom-call(f32[32,128]{1,0:T(8,128)S(1)} %copy-done.1, f32[32,128]{1,0:T(8,128)S(1)} %collective-permute-done.3.refs_1_, f32[128,128,128]{2,1,0:T(8,128)S(1)} %bitcast.1), custom_call_target="tpu_custom_call" | custom-call | flops 3221225472 | bytes 8388608 | tf_op jit(solution)/shard_map/tensor_kernel/pallas_call | solution.py:458
  9.8 0.0 collective-permute-done.2.refs_3_
  9.8 2.3 %collective-permute-done.1.refs_2_ = f32[48,128]{1,0:T(8,128)S(1)} collective-permute-done((f32[48,128]{1,0:T(8,128)S(1)}, f32[48,128]{1,0:T(8,128)S(1)}, u32[]{:S(2)}, u32[]{:S(2)}) %collective-permute-start.1) | collective-permute-done | bytes 24608 | tf_op jit(solution)/shard_map/ppermute | solution.py:427
  12.1 1.6 %collective-permute-start.4 = (f32[128,128]{1,0:T(8,128)S(1)}, f32[128,128]{1,0:T(8,128)S(1)}, u32[]{:S(2)}, u32[]{:S(2)}) collective-permute-start(f32[128,128]{1,0:T(8,128)S(1)} %get-tuple-element.39.refs_0_), channel_id=1, source_target_pairs={{0,2},{1,3},{2,0},{3,1},{4,6},{5,7},{6,4},{7,5},{8,10},{9,11},{10,... | collective-permute-start | bytes 196616 | tf_op jit(solution)/shard_map/ppermute | solution.py:427
  13.7 0.6 %collective-permute-start.6 = (f32[128,128]{1,0:T(8,128)S(1)}, f32[128,128]{1,0:T(8,128)S(1)}, u32[]{:S(2)}, u32[]{:S(2)}) collective-permute-start(f32[128,128]{1,0:T(8,128)S(1)} %get-tuple-element.40.refs_0_), channel_id=1, source_target_pairs={{0,16},{16,0},{1,17},{17,1},{2,18},{18,2},{3,19},{19,3},{4,20},{20... | collective-permute-start | bytes 196616 | tf_op jit(solution)/shard_map/ppermute | solution.py:427
  14.3 1.4 %early_kernel.1 = (f32[8192,128]{1,0:T(8,128)S(1)}, bf16[32,128,256]{2,1,0:T(8,128)(2,1)S(1)}, f32[128,128]{1,0:T(8,128)S(1)}, bf16[256,256]{1,0:T(8,128)(2,1)S(1)}) custom-call(f32[128,128]{1,0:T(8,128)S(1)} %get-tuple-element.40.refs_0_, bf16[128,128,256]{2,1,0:T(8,128)(2,1)S(1)} %get-tuple-element.41.refs_1_.refs_0_.refs_6_), custom_call_target="tpu_custom_call" | custom-call | flops 3221225472 | bytes 8388608 | tf_op jit(solution)/shard_map/early_kernel/pallas_call | solution.py:458
  15.7 0.8 %collective-permute-done.4.refs_1_ = f32[128,128]{1,0:T(8,128)S(1)} collective-permute-done((f32[128,128]{1,0:T(8,128)S(1)}, f32[128,128]{1,0:T(8,128)S(1)}, u32[]{:S(2)}, u32[]{:S(2)}) %collective-permute-start.4) | collective-permute-done | bytes 65568 | tf_op jit(solution)/shard_map/ppermute | solution.py:427
  16.5 0.1 collective-permute-start.5
  16.6 1.3 %later_kernel.1 = (f32[8192,128]{1,0:T(8,128)S(1)}, bf16[32,128,256]{2,1,0:T(8,128)(2,1)S(1)}) custom-call(bf16[128,128,256]{2,1,0:T(8,128)(2,1)S(1)} %get-tuple-element.41.refs_1_.refs_0_.refs_6_, bf16[256,256]{1,0:T(8,128)(2,1)S(1)} %get-tuple-element.44.refs_1_), custom_call_target="tpu_custom_call" | custom-call | flops 3221225472 | bytes 8388608 | tf_op jit(solution)/shard_map/later_kernel/pallas_call | solution.py:458
  17.8 0.1 collective-permute-done.6.refs_2_
  18.0 3.8 %first_kernel.1 = (f32[304,128]{1,0:T(8,128)S(1)}, f32[304,128]{1,0:T(8,128)S(1)}, f32[256,128]{1,0:T(8,128)S(1)}, f32[2,128,128]{2,1,0:T(8,128)S(1)}, f32[256,128]{1,0:T(8,128)S(1)}, /*index=5*/f32[256,128]{1,0:T(8,128)S(1)}) custom-call(f32[256,128]{1,0:T(8,128)S(1)} %stack_kernel.1.refs_0_, f32[256,128]{1,0:T(8,128)S(1)} %collective-permute-done.5.refs_1_, ...), custom_call_target="tpu_custom_call" | custom-call | flops 3221225472 | bytes 8388608 | tf_op jit(solution)/shard_map/first_kernel/pallas_call | solution.py:458
  21.8 0.4 %collective-permute-start.7 = (f32[304,128]{1,0:T(8,128)S(1)}, f32[304,128]{1,0:T(8,128)S(1)}, u32[]{:S(2)}, u32[]{:S(2)}) collective-permute-start(f32[304,128]{1,0:T(8,128)S(1)} %get-tuple-element.47), channel_id=1, source_target_pairs={{0,1},{1,0},{2,3},{3,2},{4,5},{5,4},{6,7},{7,6},{8,9},{9,8},{10,11... | collective-permute-start | bytes 466952 | tf_op jit(solution)/shard_map/ppermute | solution.py:427
  22.3 2.6 %partner_kernel.1 = (f32[160,128]{1,0:T(8,128)S(1)}, f32[96,128]{1,0:T(8,128)S(1)}, f32[8,16,128]{2,1,0:T(8,128)S(1)}, f32[8,16,128]{2,1,0:T(8,128)S(1)}) custom-call(bf16[64,128,256]{2,1,0:T(8,128)(2,1)S(1)} %get-tuple-element.50.refs_0_, bf16[32,128,256]{2,1,0:T(8,128)(2,1)S(1)} %get-tuple-element.51.refs_1_, ...), custom_call_target="tpu_custom_call" | custom-call | flops 3221225472 | bytes 8388608 | tf_op jit(solution)/shard_map/partner_kernel/pallas_call | solution.py:458
  24.8 0.7 %collective-permute-start.9 = (f32[160,128]{1,0:T(8,128)S(1)}, f32[160,128]{1,0:T(8,128)S(1)}, u32[]{:S(2)}, u32[]{:S(2)}) collective-permute-start(f32[160,128]{1,0:T(8,128)S(1)} %get-tuple-element.58), channel_id=1, source_target_pairs={{0,16},{16,0},{1,17},{17,1},{2,18},{18,2},{3,19},{19,3},{4,20},{20... | collective-permute-start | bytes 245768 | tf_op jit(solution)/shard_map/ppermute | solution.py:427
  25.5 1.5 %collective-permute-start.8 = (f32[152,128]{1,0:T(8,128)S(1)}, f32[152,128]{1,0:T(8,128)S(1)}, u32[]{:S(2)}, u32[]{:S(2)}) collective-permute-start(f32[152,128]{1,0:T(8,128)S(1)} %get-tuple-element.49), channel_id=1, source_target_pairs={{0,2},{1,3},{2,0},{3,1},{4,6},{5,7},{6,4},{7,5},{8,10},{9,11},{10,... | collective-permute-start | bytes 233480 | tf_op jit(solution)/shard_map/ppermute | solution.py:427
  27.1 2.5 %own_third_kernel.1.refs_2_ = f32[160,128]{1,0:T(8,128)S(1)} custom-call(bf16[64,128,256]{2,1,0:T(8,128)(2,1)S(1)} %get-tuple-element.50.refs_0_, bf16[32,128,256]{2,1,0:T(8,128)(2,1)S(1)} %get-tuple-element.51.refs_1_, bf16[32,128,256]{2,1,0:T(8,128)(2,1)S(1)} %get-tuple-element.52.refs_2_, f32[2,128,128]{2,1,0:T(8,128)S(1)} %get-tuple-element.53.refs_4_.refs_3_, ...), custom_call_target="tpu_custom_call" | custom-call | flops 3221225472 | bytes 8388608 | tf_op jit(solution)/shard_map/own_third_kernel/pallas_call | solution.py:458
  29.6 0.4 %collective-permute-done.8.refs_1_ = f32[152,128]{1,0:T(8,128)S(1)} collective-permute-done((f32[152,128]{1,0:T(8,128)S(1)}, f32[152,128]{1,0:T(8,128)S(1)}, u32[]{:S(2)}, u32[]{:S(2)}) %collective-permute-start.8) | collective-permute-done | bytes 77856 | tf_op jit(solution)/shard_map/ppermute | solution.py:427
  30.0 1.5 %collective-permute-start.13 = (f32[32,128]{1,0:T(8,128)S(1)}, f32[32,128]{1,0:T(8,128)S(1)}, u32[]{:S(2)}, u32[]{:S(2)}) collective-permute-start(f32[32,128]{1,0:T(8,128)S(1)} %get-tuple-element.66), channel_id=1, source_target_pairs={{0,16},{16,0},{1,17},{17,1},{2,18},{18,2},{3,19},{19,3},{4,20},{20... | collective-permute-start | bytes 49160 | tf_op jit(solution)/shard_map/ppermute | solution.py:427
  31.5 1.5 %collective-permute-start.10 = (f32[72,128]{1,0:T(8,128)S(1)}, f32[72,128]{1,0:T(8,128)S(1)}, u32[]{:S(2)}, u32[]{:S(2)}) collective-permute-start(f32[72,128]{1,0:T(8,128)S(1)} %get-tuple-element.60), channel_id=1, source_target_pairs={{0,12},{4,8},{8,4},{12,0},{1,13},{5,9},{9,5},{13,1},{2,14},{6,10},... | collective-permute-start | bytes 110600 | tf_op jit(solution)/shard_map/ppermute | solution.py:427
  33.0 0.6 %collective-permute-start.11 = (f32[72,128]{1,0:T(8,128)S(1)}, f32[72,128]{1,0:T(8,128)S(1)}, u32[]{:S(2)}, u32[]{:S(2)}) collective-permute-start(f32[72,128]{1,0:T(8,128)S(1)} %get-tuple-element.61), channel_id=1, source_target_pairs={{0,8},{4,12},{8,0},{12,4},{1,9},{5,13},{9,1},{13,5},{2,10},{6,14},... | collective-permute-start | bytes 110600 | tf_op jit(solution)/shard_map/ppermute | solution.py:427
  33.5 2.4 %collective-permute-start.12 = (f32[72,128]{1,0:T(8,128)S(1)}, f32[72,128]{1,0:T(8,128)S(1)}, u32[]{:S(2)}, u32[]{:S(2)}) collective-permute-start(f32[72,128]{1,0:T(8,128)S(1)} %get-tuple-element.62), channel_id=1, source_target_pairs={{0,4},{4,0},{8,12},{12,8},{1,5},{5,1},{9,13},{13,9},{2,6},{6,2},{1... | collective-permute-start | bytes 110600 | tf_op jit(solution)/shard_map/ppermute | solution.py:427
  35.9 0.8 %grad_b_kernel.1 = (f32[32,128]{1,0:T(8,128)}, bf16[256,256]{1,0:T(8,128)(2,1)S(1)}, bf16[256,256]{1,0:T(8,128)(2,1)S(1)}) custom-call(f32[32,128]{1,0:T(8,128)S(1)} %get-tuple-element.65.refs_0_, f32[32,128]{1,0:T(8,128)S(1)} %collective-permute-done.13.refs_1_, f32[56,128]{1,0:T(8,128)S(1)} %get-tuple-element.64.refs_2_.refs_4_, ...), custom_call_target="tpu_custom_call" | custom-call | flops 3221225472 | bytes 8388608 | tf_op jit(solution)/shard_map/grad_b_kernel/pallas_call | solution.py:458
  36.7 0.6 %collective-permute-done.10.refs_0_ = f32[72,128]{1,0:T(8,128)S(1)} collective-permute-done((f32[72,128]{1,0:T(8,128)S(1)}, f32[72,128]{1,0:T(8,128)S(1)}, u32[]{:S(2)}, u32[]{:S(2)}) %collective-permute-start.10) | collective-permute-done | bytes 36896 | tf_op jit(solution)/shard_map/ppermute | solution.py:427
  37.3 0.6 %collective-permute-done.11.refs_1_ = f32[72,128]{1,0:T(8,128)S(1)} collective-permute-done((f32[72,128]{1,0:T(8,128)S(1)}, f32[72,128]{1,0:T(8,128)S(1)}, u32[]{:S(2)}, u32[]{:S(2)}) %collective-permute-start.11) | collective-permute-done | bytes 36896 | tf_op jit(solution)/shard_map/ppermute | solution.py:427
  37.8 0.4 collective-permute-done.12.refs_2_
  38.2 0.8 %last_kernel.1 = (f32[16,128]{1,0:T(8,128)}, f32[32,128]{1,0:T(8,128)}) custom-call(f32[72,128]{1,0:T(8,128)S(1)} %collective-permute-done.10.refs_0_, f32[72,128]{1,0:T(8,128)S(1)} %collective-permute-done.11.refs_1_, f32[72,128]{1,0:T(8,128)S(1)} %collective-permute-done.12.refs_2_, f32[72,128]{1,0:T(8,128)S(1)} %get-tuple-element.63.refs_3_, ...), custom_call_target="tpu_custom_call" | custom-call | tf_op jit(solution)/shard_map/last_kernel/pallas_call | solution.py:458
  (21 shorter events, 0.1 us)
Async XLA Ops:
  0.6 3.1 %copy-start = (f32[32,128]{1,0:T(8,128)S(1)}, f32[32,128]{1,0:T(8,128)}, u32[]{:S(2)}) copy-start(f32[32,128]{1,0:T(8,128)} %refs_1_.1) | copy-start | bytes 49156
  0.6 3.1 %copy-start.2 = (f32[16,128]{1,0:T(8,128)S(1)}, f32[16,128]{1,0:T(8,128)}, u32[]{:S(2)}) copy-start(f32[16,128]{1,0:T(8,128)} %refs_0_.2) | copy-start | bytes 24580
  0.7 7.5 %collective-permute-start.3 = (f32[32,128]{1,0:T(8,128)}, f32[32,128]{1,0:T(8,128)S(1)}, u32[]{:S(2)}, u32[]{:S(2)}) collective-permute-start(f32[32,128]{1,0:T(8,128)} %refs_0_.3), channel_id=1, source_target_pairs={{0,16},{16,0},{1,17},{17,1},{2,18},{18,2},{3,19},{19,3},{4,20},{20... | collective-permute-start | bytes 49160 | tf_op jit(solution)/shard_map/ppermute | solution.py:427
  3.7 4.5 %slice-start = ((s8[8388608]{0:T(1024)(128)(4,1)}), s8[4194304]{0:T(1024)(128)(4,1)S(1)}, s32[]{:S(2)}) async-start(s8[8388608]{0:T(1024)(128)(4,1)} %bitcast), calls=%async_computation | async-start | bytes 8388608
  3.7 4.5 %slice-start.1 = ((s8[8388608]{0:T(1024)(128)(4,1)}), s8[4194304]{0:T(1024)(128)(4,1)S(1)}, s32[]{:S(2)}) async-start(s8[8388608]{0:T(1024)(128)(4,1)} %bitcast), calls=%async_computation.1 | async-start | bytes 8388608
  3.7 4.5 %copy-start.1 = (f32[32,128]{1,0:T(8,128)S(1)}, f32[32,128]{1,0:T(8,128)}, u32[]{:S(2)}) copy-start(f32[32,128]{1,0:T(8,128)} %refs_0_.3) | copy-start | bytes 49156
  3.7 6.1 %collective-permute-start.2 = (f32[48,128]{1,0:T(8,128)S(1)}, f32[48,128]{1,0:T(8,128)S(1)}, u32[]{:S(2)}, u32[]{:S(2)}) collective-permute-start(f32[48,128]{1,0:T(8,128)S(1)} %own_kernel.1.refs_0_), channel_id=1, source_target_pairs={{0,12},{4,8},{8,4},{12,0},{1,13},{5,9},{9,5},{13,1},{2,14},{6,10},... | collective-permute-start | bytes 73736 | tf_op jit(solution)/shard_map/ppermute | solution.py:427
  7.4 4.7 %collective-permute-start.1 = (f32[48,128]{1,0:T(8,128)S(1)}, f32[48,128]{1,0:T(8,128)S(1)}, u32[]{:S(2)}, u32[]{:S(2)}) collective-permute-start(f32[48,128]{1,0:T(8,128)S(1)} %own_kernel.1.refs_0_), channel_id=1, source_target_pairs={{0,8},{4,12},{8,0},{12,4},{1,9},{5,13},{9,1},{13,5},{2,10},{6,14},... | collective-permute-start | bytes 73736 | tf_op jit(solution)/shard_map/ppermute | solution.py:427
  7.4 4.7 %collective-permute-start = (f32[48,128]{1,0:T(8,128)S(1)}, f32[48,128]{1,0:T(8,128)S(1)}, u32[]{:S(2)}, u32[]{:S(2)}) collective-permute-start(f32[48,128]{1,0:T(8,128)S(1)} %own_kernel.1.refs_0_), channel_id=1, source_target_pairs={{0,4},{4,0},{8,12},{12,8},{1,5},{5,1},{9,13},{13,9},{2,6},{6,2},{1... | collective-permute-start | bytes 73736 | tf_op jit(solution)/shard_map/ppermute | solution.py:427
  12.1 4.3 %collective-permute-start.4 = (f32[128,128]{1,0:T(8,128)S(1)}, f32[128,128]{1,0:T(8,128)S(1)}, u32[]{:S(2)}, u32[]{:S(2)}) collective-permute-start(f32[128,128]{1,0:T(8,128)S(1)} %get-tuple-element.39.refs_0_), channel_id=1, source_target_pairs={{0,2},{1,3},{2,0},{3,1},{4,6},{5,7},{6,4},{7,5},{8,10},{9,11},{10,... | collective-permute-start | bytes 196616 | tf_op jit(solution)/shard_map/ppermute | solution.py:427
  13.7 4.3 %collective-permute-start.6 = (f32[128,128]{1,0:T(8,128)S(1)}, f32[128,128]{1,0:T(8,128)S(1)}, u32[]{:S(2)}, u32[]{:S(2)}) collective-permute-start(f32[128,128]{1,0:T(8,128)S(1)} %get-tuple-element.40.refs_0_), channel_id=1, source_target_pairs={{0,16},{16,0},{1,17},{17,1},{2,18},{18,2},{3,19},{19,3},{4,20},{20... | collective-permute-start | bytes 196616 | tf_op jit(solution)/shard_map/ppermute | solution.py:427
  16.5 1.5 %collective-permute-start.5 = (f32[256,128]{1,0:T(8,128)S(1)}, f32[256,128]{1,0:T(8,128)S(1)}, u32[]{:S(2)}, u32[]{:S(2)}) collective-permute-start(f32[256,128]{1,0:T(8,128)S(1)} %stack_kernel.1.refs_0_), channel_id=1, source_target_pairs={{0,1},{1,0},{2,3},{3,2},{4,5},{5,4},{6,7},{7,6},{8,9},{9,8},{10,11... | collective-permute-start | bytes 393224 | tf_op jit(solution)/shard_map/ppermute | solution.py:427
  21.8 3.7 %collective-permute-start.7 = (f32[304,128]{1,0:T(8,128)S(1)}, f32[304,128]{1,0:T(8,128)S(1)}, u32[]{:S(2)}, u32[]{:S(2)}) collective-permute-start(f32[304,128]{1,0:T(8,128)S(1)} %get-tuple-element.47), channel_id=1, source_target_pairs={{0,1},{1,0},{2,3},{3,2},{4,5},{5,4},{6,7},{7,6},{8,9},{9,8},{10,11... | collective-permute-start | bytes 466952 | tf_op jit(solution)/shard_map/ppermute | solution.py:427
  24.8 4.8 %collective-permute-start.9 = (f32[160,128]{1,0:T(8,128)S(1)}, f32[160,128]{1,0:T(8,128)S(1)}, u32[]{:S(2)}, u32[]{:S(2)}) collective-permute-start(f32[160,128]{1,0:T(8,128)S(1)} %get-tuple-element.58), channel_id=1, source_target_pairs={{0,16},{16,0},{1,17},{17,1},{2,18},{18,2},{3,19},{19,3},{4,20},{20... | collective-permute-start | bytes 245768 | tf_op jit(solution)/shard_map/ppermute | solution.py:427
  25.5 4.5 %collective-permute-start.8 = (f32[152,128]{1,0:T(8,128)S(1)}, f32[152,128]{1,0:T(8,128)S(1)}, u32[]{:S(2)}, u32[]{:S(2)}) collective-permute-start(f32[152,128]{1,0:T(8,128)S(1)} %get-tuple-element.49), channel_id=1, source_target_pairs={{0,2},{1,3},{2,0},{3,1},{4,6},{5,7},{6,4},{7,5},{8,10},{9,11},{10,... | collective-permute-start | bytes 233480 | tf_op jit(solution)/shard_map/ppermute | solution.py:427
  30.0 5.9 %collective-permute-start.13 = (f32[32,128]{1,0:T(8,128)S(1)}, f32[32,128]{1,0:T(8,128)S(1)}, u32[]{:S(2)}, u32[]{:S(2)}) collective-permute-start(f32[32,128]{1,0:T(8,128)S(1)} %get-tuple-element.66), channel_id=1, source_target_pairs={{0,16},{16,0},{1,17},{17,1},{2,18},{18,2},{3,19},{19,3},{4,20},{20... | collective-permute-start | bytes 49160 | tf_op jit(solution)/shard_map/ppermute | solution.py:427
  31.5 5.8 %collective-permute-start.10 = (f32[72,128]{1,0:T(8,128)S(1)}, f32[72,128]{1,0:T(8,128)S(1)}, u32[]{:S(2)}, u32[]{:S(2)}) collective-permute-start(f32[72,128]{1,0:T(8,128)S(1)} %get-tuple-element.60), channel_id=1, source_target_pairs={{0,12},{4,8},{8,4},{12,0},{1,13},{5,9},{9,5},{13,1},{2,14},{6,10},... | collective-permute-start | bytes 110600 | tf_op jit(solution)/shard_map/ppermute | solution.py:427
  33.0 4.9 %collective-permute-start.11 = (f32[72,128]{1,0:T(8,128)S(1)}, f32[72,128]{1,0:T(8,128)S(1)}, u32[]{:S(2)}, u32[]{:S(2)}) collective-permute-start(f32[72,128]{1,0:T(8,128)S(1)} %get-tuple-element.61), channel_id=1, source_target_pairs={{0,8},{4,12},{8,0},{12,4},{1,9},{5,13},{9,1},{13,5},{2,10},{6,14},... | collective-permute-start | bytes 110600 | tf_op jit(solution)/shard_map/ppermute | solution.py:427
  33.5 4.7 %collective-permute-start.12 = (f32[72,128]{1,0:T(8,128)S(1)}, f32[72,128]{1,0:T(8,128)S(1)}, u32[]{:S(2)}, u32[]{:S(2)}) collective-permute-start(f32[72,128]{1,0:T(8,128)S(1)} %get-tuple-element.62), channel_id=1, source_target_pairs={{0,4},{4,0},{8,12},{12,8},{1,5},{5,1},{9,13},{13,9},{2,6},{6,2},{1... | collective-permute-start | bytes 110600 | tf_op jit(solution)/shard_map/ppermute | solution.py:427
